TPU v7x, 512 devices: a whole 4x4x16 slice. The times are simulated.
512 devices in a mesh: row: 64 (over z, y), col: 8 (over x, core).
Axes of the slice: x: 4, y: 4, z: 16, core: 2. Of those that a mesh axis runs over, the one named last changes fastest.
Arguments:
- activations: bfloat16 [131072, 8192], P('row', 'col'), may hold values from -640 to 640
- start_basis: bfloat16 [8192, 256], P('col'), may hold values from -0.0625 to 0.0625
Outputs:
- basis: bfloat16 [131072, 256], P('row', 'col')
- projected: float32 [256, 8192], P('row', 'col')
All inputs are finite; a program needn't handle non-finite values.
Results may differ from a plain program's by a relative error of at most 0.023.
Values may be sent and summed in bfloat16 or wider, within the bound.
No kernel may reach another device: no remote copies, remote signals or barrier semaphores. Data moves between devices by JAX's collectives and lax.ppermute only.
A program may use at most 64 MiB of HBM per device.

v0:
```python
import math

import jax
import jax.numpy as jnp
from jax import lax
from jax.sharding import PartitionSpec as P


def partner_2(value, axis, distance):
    mask = 2**distance
    pairs = [(source, source ^ mask) for source in range(lax.axis_size(axis))]
    return lax.ppermute(value, axis, pairs)


def inner_product(matrix):
    return lax.dot_general(
        matrix,
        matrix,
        (((0,), (0,)), ((), ())),
        precision=lax.Precision.HIGHEST,
        preferred_element_type=jnp.float32,
    )


def right_solve(lower_factor, sketch):
    return lax.linalg.triangular_solve(
        lower_factor, sketch, left_side=False, lower=True, transpose_a=True
    )


def local(activations, start_basis):
    rows_dev = activations.shape[0]
    rank_width = start_basis.shape[1]
    root_tokens = math.sqrt(rows_dev * lax.axis_size("row"))
    partial_value = jnp.dot(activations, start_basis, preferred_element_type=jnp.float32)
    summed = lax.psum(partial_value, "col")
    upper_factor = jnp.linalg.cholesky(inner_product(summed)).T
    for level_bit in range(lax.axis_size("row").bit_length() - 1):
        partner = partner_2(upper_factor, "row", level_bit)
        upper_factor = jnp.linalg.cholesky(inner_product(upper_factor) + inner_product(partner)).T
    basis_full = (right_solve(upper_factor.T, summed) * root_tokens).astype(jnp.bfloat16)
    projected = lax.psum_scatter(
        lax.dot_general(
            basis_full, activations, (((0,), (0,)), ((), ())), preferred_element_type=jnp.float32
        )
        / root_tokens,
        "row",
        scatter_dimension=0,
        tiled=True,
    )
    col_width = rank_width // lax.axis_size("col")
    basis = lax.dynamic_slice_in_dim(basis_full, lax.axis_index("col") * col_width, col_width, 1)
    return (basis, projected)


def solution(mesh):
    return jax.shard_map(
        local,
        mesh=mesh,
        in_specs=(P("row", "col"), P("col", None)),
        out_specs=(P("row", "col"), P("row", "col")),
        check_vma=False,
    )
```

profile of v0, /device:TPU:2, one launch (start us, length us, event | category | flops | bytes accessed | tf_op | source)
XLA Modules:
  0.0 776.9 jit_solution(10005166845684133330)
XLA Ops:
  7.2 1.0 copy-done
  8.2 4.7 fusion.100
  13.0 83.3 %all-reduce.5.cloned.1.call-done = f32[2048,256]{1,0:T(8,128)} async-done(((f32[2048,256]{1,0:T(8,128)}), f32[2048,256]{1,0:T(8,128)}) %all-reduce.5.cloned.1.call-update) | async-done | bytes 2097168 | tf_op jit(solution)/shard_map/psum | solution.py:36
  96.3 5.7 fusion.101
  102.2 11.7 %cholesky.340 = f32[128,128]{1,0:T(8,128)S(1)} custom-call(f32[128,128]{1,0:T(8,128)S(1)} %cholesky.574), custom_call_target="Cholesky" | custom-call | tf_op jit(solution)/shard_map/jit(cholesky)/cholesky | solution.py:37
  113.9 9.8 %custom-call.18 = f32[1,128,128]{1,2,0:T(8,128)S(1)} custom-call(f32[1,128,128]{2,1,0:T(8,128)S(1)} %get-tuple-element.48), custom_call_target="InvertDiagBlocksLowerTriangular" | custom-call | tf_op jit(solution)/shard_map/jit(cholesky)/cholesky | solution.py:37
  124.2 12.0 %cholesky.357 = f32[128,128]{1,0:T(8,128)S(1)} custom-call(f32[128,128]{1,0:T(8,128)S(1)} %convolution_subtract_fusion.1), custom_call_target="Cholesky" | custom-call | tf_op jit(solution)/shard_map/jit(cholesky)/cholesky | solution.py:37
  136.3 0.6 compare_reduce_fusion.12
  138.3 3.4 collective-permute-start
  142.1 4.8 collective-permute-done
  147.6 11.7 %cholesky.374 = f32[128,128]{1,0:T(8,128)S(1)} custom-call(f32[128,128]{1,0:T(8,128)S(1)} %cholesky.577), custom_call_target="Cholesky" | custom-call | tf_op jit(solution)/shard_map/jit(cholesky)/cholesky | solution.py:40
  159.3 9.8 %custom-call.19 = f32[1,128,128]{1,2,0:T(8,128)S(1)} custom-call(f32[1,128,128]{2,1,0:T(8,128)S(1)} %get-tuple-element.44), custom_call_target="InvertDiagBlocksLowerTriangular" | custom-call | tf_op jit(solution)/shard_map/jit(cholesky)/cholesky | solution.py:40
  169.6 11.7 %cholesky.391 = f32[128,128]{1,0:T(8,128)S(1)} custom-call(f32[128,128]{1,0:T(8,128)S(1)} %slice_subtract_fusion.5), custom_call_target="Cholesky" | custom-call | tf_op jit(solution)/shard_map/jit(cholesky)/cholesky | solution.py:40
  181.4 0.6 compare_reduce_fusion.10
  182.0 0.6 compare_reduce_fusion.11
  184.0 5.1 collective-permute-start.1
  189.5 4.2 collective-permute-done.1
  194.4 11.7 %cholesky.408 = f32[128,128]{1,0:T(8,128)S(1)} custom-call(f32[128,128]{1,0:T(8,128)S(1)} %cholesky.580), custom_call_target="Cholesky" | custom-call | tf_op jit(solution)/shard_map/jit(cholesky)/cholesky | solution.py:40
  206.2 9.8 %custom-call.20 = f32[1,128,128]{1,2,0:T(8,128)S(1)} custom-call(f32[1,128,128]{2,1,0:T(8,128)S(1)} %get-tuple-element.40), custom_call_target="InvertDiagBlocksLowerTriangular" | custom-call | tf_op jit(solution)/shard_map/jit(cholesky)/cholesky | solution.py:40
  216.5 11.7 %cholesky.425 = f32[128,128]{1,0:T(8,128)S(1)} custom-call(f32[128,128]{1,0:T(8,128)S(1)} %slice_subtract_fusion.4), custom_call_target="Cholesky" | custom-call | tf_op jit(solution)/shard_map/jit(cholesky)/cholesky | solution.py:40
  228.2 0.6 compare_reduce_fusion.8
  228.8 0.6 compare_reduce_fusion.9
  230.8 3.7 collective-permute-start.2
  234.9 4.2 collective-permute-done.2
  239.7 11.7 %cholesky.442 = f32[128,128]{1,0:T(8,128)S(1)} custom-call(f32[128,128]{1,0:T(8,128)S(1)} %cholesky.583), custom_call_target="Cholesky" | custom-call | tf_op jit(solution)/shard_map/jit(cholesky)/cholesky | solution.py:40
  251.5 9.8 %custom-call.21 = f32[1,128,128]{1,2,0:T(8,128)S(1)} custom-call(f32[1,128,128]{2,1,0:T(8,128)S(1)} %get-tuple-element.36), custom_call_target="InvertDiagBlocksLowerTriangular" | custom-call | tf_op jit(solution)/shard_map/jit(cholesky)/cholesky | solution.py:40
  261.8 11.7 %cholesky.459 = f32[128,128]{1,0:T(8,128)S(1)} custom-call(f32[128,128]{1,0:T(8,128)S(1)} %slice_subtract_fusion.3), custom_call_target="Cholesky" | custom-call | tf_op jit(solution)/shard_map/jit(cholesky)/cholesky | solution.py:40
  273.5 0.6 compare_reduce_fusion.6
  274.2 0.6 compare_reduce_fusion.7
  276.1 4.9 collective-permute-start.3
  281.4 6.7 collective-permute-done.3
  288.7 11.7 %cholesky.476 = f32[128,128]{1,0:T(8,128)S(1)} custom-call(f32[128,128]{1,0:T(8,128)S(1)} %cholesky.586), custom_call_target="Cholesky" | custom-call | tf_op jit(solution)/shard_map/jit(cholesky)/cholesky | solution.py:40
  300.5 9.8 %custom-call.22 = f32[1,128,128]{1,2,0:T(8,128)S(1)} custom-call(f32[1,128,128]{2,1,0:T(8,128)S(1)} %get-tuple-element.32), custom_call_target="InvertDiagBlocksLowerTriangular" | custom-call | tf_op jit(solution)/shard_map/jit(cholesky)/cholesky | solution.py:40
  310.8 11.7 %cholesky.493 = f32[128,128]{1,0:T(8,128)S(1)} custom-call(f32[128,128]{1,0:T(8,128)S(1)} %slice_subtract_fusion.2), custom_call_target="Cholesky" | custom-call | tf_op jit(solution)/shard_map/jit(cholesky)/cholesky | solution.py:40
  322.5 0.6 compare_reduce_fusion.4
  323.2 0.6 compare_reduce_fusion.5
  325.1 7.8 %collective-permute-start.4 = (f32[256,256]{0,1:T(8,128)S(1)}, f32[256,256]{0,1:T(8,128)S(1)}, u32[]{:S(2)}, u32[]{:S(2)}) collective-permute-start(f32[256,256]{0,1:T(8,128)S(1)} %fusion.18), channel_id=1, source_target_pairs={{0,128},{8,136},{16,144},{24,152},{32,160},{40,168},{48,176},{56,1... | collective-permute-start | bytes 786440 | tf_op jit(solution)/shard_map/ppermute | solution.py:12
  333.4 16.2 %collective-permute-done.4 = f32[256,256]{0,1:T(8,128)S(1)} collective-permute-done((f32[256,256]{0,1:T(8,128)S(1)}, f32[256,256]{0,1:T(8,128)S(1)}, u32[]{:S(2)}, u32[]{:S(2)}) %collective-permute-start.4) | collective-permute-done | bytes 262176 | tf_op jit(solution)/shard_map/ppermute | solution.py:12
  350.2 11.7 %cholesky.510 = f32[128,128]{1,0:T(8,128)S(1)} custom-call(f32[128,128]{1,0:T(8,128)S(1)} %cholesky.589), custom_call_target="Cholesky" | custom-call | tf_op jit(solution)/shard_map/jit(cholesky)/cholesky | solution.py:40
  361.9 9.8 %custom-call.23 = f32[1,128,128]{1,2,0:T(8,128)S(1)} custom-call(f32[1,128,128]{2,1,0:T(8,128)S(1)} %get-tuple-element.28), custom_call_target="InvertDiagBlocksLowerTriangular" | custom-call | tf_op jit(solution)/shard_map/jit(cholesky)/cholesky | solution.py:40
  372.2 11.7 %cholesky.527 = f32[128,128]{1,0:T(8,128)S(1)} custom-call(f32[128,128]{1,0:T(8,128)S(1)} %slice_subtract_fusion.1), custom_call_target="Cholesky" | custom-call | tf_op jit(solution)/shard_map/jit(cholesky)/cholesky | solution.py:40
  384.0 0.6 compare_reduce_fusion.2
  384.6 0.6 compare_reduce_fusion.3
  386.6 11.4 %collective-permute-start.5 = (f32[256,256]{0,1:T(8,128)S(1)}, f32[256,256]{0,1:T(8,128)S(1)}, u32[]{:S(2)}, u32[]{:S(2)}) collective-permute-start(f32[256,256]{0,1:T(8,128)S(1)} %fusion.20), channel_id=1, source_target_pairs={{0,256},{8,264},{16,272},{24,280},{32,288},{40,296},{48,304},{56,3... | collective-permute-start | bytes 786440 | tf_op jit(solution)/shard_map/ppermute | solution.py:12
  398.5 19.7 %collective-permute-done.5 = f32[256,256]{0,1:T(8,128)S(1)} collective-permute-done((f32[256,256]{0,1:T(8,128)S(1)}, f32[256,256]{0,1:T(8,128)S(1)}, u32[]{:S(2)}, u32[]{:S(2)}) %collective-permute-start.5) | collective-permute-done | bytes 262176 | tf_op jit(solution)/shard_map/ppermute | solution.py:12
  418.8 11.7 %cholesky.544 = f32[128,128]{1,0:T(8,128)S(1)} custom-call(f32[128,128]{1,0:T(8,128)S(1)} %cholesky.592), custom_call_target="Cholesky" | custom-call | tf_op jit(solution)/shard_map/jit(cholesky)/cholesky | solution.py:40
  430.6 9.8 %custom-call.24 = f32[1,128,128]{1,2,0:T(8,128)S(1)} custom-call(f32[1,128,128]{2,1,0:T(8,128)S(1)} %get-tuple-element.24), custom_call_target="InvertDiagBlocksLowerTriangular" | custom-call | tf_op jit(solution)/shard_map/jit(cholesky)/cholesky | solution.py:40
  440.9 11.7 %cholesky.561 = f32[128,128]{1,0:T(8,128)S(1)} custom-call(f32[128,128]{1,0:T(8,128)S(1)} %slice_subtract_fusion), custom_call_target="Cholesky" | custom-call | tf_op jit(solution)/shard_map/jit(cholesky)/cholesky | solution.py:40
  452.6 0.6 compare_reduce_fusion
  453.3 0.6 compare_reduce_fusion.1
  455.3 4.2 while.1
  455.6 0.6 fusion.137
  456.1 1.4 bitcast_dynamic-update-slice_fusion.2
  458.1 1.4 bitcast_dynamic-update-slice_fusion.2
  459.5 19.7 %custom-call.11 = f32[2,128,128]{1,2,0:T(8,128)S(1)} custom-call(f32[2,128,128]{2,1,0:T(8,128)S(1)} %get-tuple-element.10), custom_call_target="InvertDiagBlocksLowerTriangular" | custom-call | tf_op jit(solution)/shard_map/triangular_solve | solution.py:26
  479.2 1.1 fusion.1
  480.3 1.8 convolution_subtract_fusion
  482.1 1.1 fusion.40
  483.4 0.9 copy-done.2
  484.3 2.3 convolution_multiply_fusion
  486.6 1.3 dynamic-slice.3
  488.6 0.7 constant_dynamic-slice_fusion.1
  489.2 279.1 %all-reduce.7.cloned.1.call-done = f32[256,1024]{1,0:T(8,128)} async-done(((f32[256,1024]{1,0:T(8,128)}), f32[256,1024]{1,0:T(8,128)}) %all-reduce.7.cloned.1.call-update) | async-done | bytes 1048592
  768.3 1.4 constant_dynamic-slice_fusion.2
  (90 shorter events, 11.3 us)
Async XLA Ops:
  7.2 1.0 copy-start
  7.2 89.1 %all-reduce.5.cloned.1.call-start = ((), (), s32[]{:S(2)}) async-start(), calls=%async_computation | async-start | bytes 4194304 | tf_op jit(solution)/shard_map/psum | solution.py:36
  13.0 755.3 %all-reduce.7.cloned.1.call-start = ((), (), s32[]{:S(2)}) async-start(), calls=%async_computation.1 | async-start | bytes 2097152
  138.3 8.7 %collective-permute-start = (f32[256,256]{0,1:T(8,128)S(1)}, f32[256,256]{0,1:T(8,128)S(1)}, u32[]{:S(2)}, u32[]{:S(2)}) collective-permute-start(f32[256,256]{0,1:T(8,128)S(1)} %fusion.10), channel_id=1, source_target_pairs={{0,8},{8,0},{16,24},{24,16},{32,40},{40,32},{48,56},{56,48},{64,72... | collective-permute-start | bytes 786440 | tf_op jit(solution)/shard_map/ppermute | solution.py:12
  184.0 9.8 %collective-permute-start.1 = (f32[256,256]{0,1:T(8,128)S(1)}, f32[256,256]{0,1:T(8,128)S(1)}, u32[]{:S(2)}, u32[]{:S(2)}) collective-permute-start(f32[256,256]{0,1:T(8,128)S(1)} %fusion.12), channel_id=1, source_target_pairs={{0,16},{8,24},{16,0},{24,8},{32,48},{40,56},{48,32},{56,40},{64,80... | collective-permute-start | bytes 786440 | tf_op jit(solution)/shard_map/ppermute | solution.py:12
  230.8 8.3 %collective-permute-start.2 = (f32[256,256]{0,1:T(8,128)S(1)}, f32[256,256]{0,1:T(8,128)S(1)}, u32[]{:S(2)}, u32[]{:S(2)}) collective-permute-start(f32[256,256]{0,1:T(8,128)S(1)} %fusion.14), channel_id=1, source_target_pairs={{0,32},{8,40},{16,48},{24,56},{32,0},{40,8},{48,16},{56,24},{64,96... | collective-permute-start | bytes 786440 | tf_op jit(solution)/shard_map/ppermute | solution.py:12
  276.1 12.0 %collective-permute-start.3 = (f32[256,256]{0,1:T(8,128)S(1)}, f32[256,256]{0,1:T(8,128)S(1)}, u32[]{:S(2)}, u32[]{:S(2)}) collective-permute-start(f32[256,256]{0,1:T(8,128)S(1)} %fusion.16), channel_id=1, source_target_pairs={{0,64},{8,72},{16,80},{24,88},{32,96},{40,104},{48,112},{56,120},{... | collective-permute-start | bytes 786440 | tf_op jit(solution)/shard_map/ppermute | solution.py:12
  325.1 24.4 %collective-permute-start.4 = (f32[256,256]{0,1:T(8,128)S(1)}, f32[256,256]{0,1:T(8,128)S(1)}, u32[]{:S(2)}, u32[]{:S(2)}) collective-permute-start(f32[256,256]{0,1:T(8,128)S(1)} %fusion.18), channel_id=1, source_target_pairs={{0,128},{8,136},{16,144},{24,152},{32,160},{40,168},{48,176},{56,1... | collective-permute-start | bytes 786440 | tf_op jit(solution)/shard_map/ppermute | solution.py:12
  386.6 31.6 %collective-permute-start.5 = (f32[256,256]{0,1:T(8,128)S(1)}, f32[256,256]{0,1:T(8,128)S(1)}, u32[]{:S(2)}, u32[]{:S(2)}) collective-permute-start(f32[256,256]{0,1:T(8,128)S(1)} %fusion.20), channel_id=1, source_target_pairs={{0,256},{8,264},{16,272},{24,280},{32,288},{40,296},{48,304},{56,3... | collective-permute-start | bytes 786440 | tf_op jit(solution)/shard_map/ppermute | solution.py:12
  418.6 60.5 %copy-start.1 = (f32[2048,256]{1,0:T(8,128)S(1)}, f32[2048,256]{1,0:T(8,128)}, u32[]{:S(2)}) copy-start(f32[2048,256]{1,0:T(8,128)} %all-reduce.5.cloned.1.call-done) | copy-start | bytes 6291460
  482.1 2.2 copy-start.2
Sparse Core Ops, SparseCore 0:
  13.1 83.1 all-reduce.4
  486.8 281.4 all-reduce.6
where the time goes:
time: 787 us; the launch traced here: 777 us
  waiting for transfers between devices  418 us (53%)
  other arithmetic  262 us (33%)
  starting transfers between devices  36.3 us (5%)
  matrix products  25 us (3%)
  between operations  24.8 us (3%)
  local copies, waits for them, and re-layouts  10.2 us (1%)
    unnamed x3, waiting for transfers between devices  279 us
    another operation x42, other arithmetic, local(): jnp.linalg.cholesky(inner_product(upper_factor) + inner_product(partner))  207 us
    psum x1, waiting for transfers between devices, local(): summed = lax.psum(partial_value, 'col')  83.3 us
    ppermute x6, waiting for transfers between devices, partner_2(): return lax.ppermute(value, axis, pairs)  55.8 us
    ppermute x6, starting transfers between devices, partner_2(): return lax.ppermute(value, axis, pairs)  36.3 us
    another operation x6, other arithmetic, local(): upper_factor = jnp.linalg.cholesky(inner_product(summed)).T  34.3 us
    another operation x3, other arithmetic, right_solve(): lax.linalg.triangular_solve(lower_factor, sketch, left_side=False, lower=...  19.7 us
  transfers between devices with their start and end apart: 8, of which 8 were waited for; matrix products, arithmetic and copies ran while one was open for 1% of the time, Pallas kernels for 0%

commit v1 on v0

v1 whole, which is shorter than its diff:
```python
import math

import jax
import jax.numpy as jnp
from jax import lax
from jax.sharding import PartitionSpec as P

Y = 4


def groups(rows, cols):
    depth = rows // Y
    plane = [[(z * Y + y) * cols + c for y in range(Y) for c in range(cols)] for z in range(depth)]
    along_z = [[z * Y + y for z in range(depth)] for y in range(Y)]
    return plane, along_z


def exchange(blocks, axis, members=None):
    return lax.all_to_all(blocks, axis, 0, 0, axis_index_groups=members)


def share(block, count, axis, members=None):
    return exchange(jnp.broadcast_to(block[None], (count,) + block.shape), axis, members)


def local(activations, start_basis):
    rows, cols = lax.axis_size("row"), lax.axis_size("col")
    rows_dev, rank = activations.shape[0], start_basis.shape[1]
    root_tokens = math.sqrt(rows_dev * rows)
    plane, along_z = groups(rows, cols)
    plane_size, depth = Y * cols, rows // Y

    partial = jnp.dot(activations, start_basis, preferred_element_type=jnp.float32)
    partial = partial.astype(jnp.bfloat16).reshape(cols, rows_dev // cols, rank)
    own = jnp.sum(exchange(partial, "col").astype(jnp.float32), 0).astype(jnp.bfloat16)
    sketch = share(own, cols, "col").reshape(rows_dev, rank)

    gram = lax.dot_general(own, own, (((0,), (0,)), ((), ())), preferred_element_type=jnp.float32)
    gram = gram.reshape(plane_size, rank // plane_size, rank)
    gram = jnp.sum(exchange(gram, ("row", "col"), plane), 0)
    gram = jnp.sum(share(gram, depth, "row", along_z), 0)
    gram = share(gram, plane_size, ("row", "col"), plane).reshape(rank, rank)

    lower = lax.linalg.cholesky(gram, symmetrize_input=False)
    inverse = lax.linalg.triangular_solve(
        lower, jnp.eye(rank, dtype=jnp.float32), left_side=True, lower=True
    )
    inverse = inverse * root_tokens
    high = inverse.astype(jnp.bfloat16)
    low = (inverse - high.astype(jnp.float32)).astype(jnp.bfloat16)
    by_rows = (((1,), (1,)), ((), ()))
    basis = lax.dot_general(sketch, high, by_rows, preferred_element_type=jnp.float32)
    basis = basis + lax.dot_general(sketch, low, by_rows, preferred_element_type=jnp.float32)
    basis = basis.astype(jnp.bfloat16)

    projected = lax.dot_general(
        basis, activations, (((0,), (0,)), ((), ())), preferred_element_type=jnp.float32
    )
    projected = projected.astype(jnp.bfloat16).reshape(rows, rank // rows, -1)
    projected = jnp.sum(exchange(projected, "row").astype(jnp.float32), 0) / root_tokens

    width = rank // cols
    basis = lax.dynamic_slice_in_dim(basis, lax.axis_index("col") * width, width, 1)
    return (basis, projected)


def solution(mesh):
    return jax.shard_map(
        local,
        mesh=mesh,
        in_specs=(P("row", "col"), P("col", None)),
        out_specs=(P("row", "col"), P("row", "col")),
        check_vma=False,
    )
```

time: 787 us -> 194 us (0.25)
  the two profiles are of different devices: /device:TPU:2 before, /device:TPU:8 now
where the time goes in v1:
time: 194 us; the launch traced here: 193 us
  blocking collectives  62.1 us (32%)
  other arithmetic  55 us (28%)
  waiting for transfers between devices  40.2 us (21%)
  starting transfers between devices  16.6 us (9%)
  local copies, waits for them, and re-layouts  9.94 us (5%)
  matrix products  7.18 us (4%)
  between operations  2.19 us (1%)
    all_to_all x3, blocking collectives, exchange(): return lax.all_to_all(blocks, axis, 0, 0, axis_index_groups=members)  62.1 us
    all_to_all x3, waiting for transfers between devices, exchange(): return lax.all_to_all(blocks, axis, 0, 0, axis_index_groups=members)  40.2 us
    another operation x6, other arithmetic, local(): lower = lax.linalg.cholesky(gram, symmetrize_input=False)  34 us
    another operation x3, other arithmetic, local(): lax.linalg.triangular_solve(lower, jnp.eye(rank, dtype=jnp.float32), left...  19.9 us
    all_to_all x3, starting transfers between devices, exchange(): return lax.all_to_all(blocks, axis, 0, 0, axis_index_groups=members)  16.6 us
    another operation x6, local copies, waits for them, and re-layouts  4.06 us
  transfers between devices with their start and end apart: 3, of which 2 were waited for; matrix products, arithmetic and copies ran while one was open for 31% of the time, Pallas kernels for 0%

profile of v1, /device:TPU:8, one launch (start us, length us, event | category | flops | bytes accessed | tf_op | source)
XLA Modules:
  0.0 193.3 jit_solution(14717521763451712154)
XLA Ops:
  0.6 0.0 copy-start
  0.6 1.0 copy-done
  1.7 3.4 %convolution_convert_fusion = bf16[2048,256]{1,0:T(8,128)(2,1)S(1)} fusion(bf16[2048,1024]{1,0:T(8,128)(2,1)} %param.2, bf16[1024,256]{1,0:T(8,128)(2,1)S(1)} %copy-done), kind=kOutput, calls=%fused_computation.4 | convolution fusion | flops 1074266112 | bytes 5767168 | tf_op jit(solution)/shard_map/dot_general | solution.py:33
  5.1 20.2 %all_to_all.30 = bf16[8,256,256]{2,1,0:T(8,128)(2,1)S(1)} all-to-all(bf16[8,256,256]{2,1,0:T(8,128)(2,1)S(1)} %bitcast.46), channel_id=1, replica_groups=mesh['row'=64,'col'=8] {'col'}, dimensions={0} | all-to-all | bytes 2097152 | tf_op jit(solution)/shard_map/all_to_all | solution.py:19
  25.3 0.1 reduce_sum.39
  25.5 0.1 copy.5
  25.6 0.2 fusion.4
  25.8 14.4 %all_to_all.31 = f32[32,8,256]{2,1,0:T(8,128)S(1)} all-to-all(f32[32,8,256]{2,1,0:T(8,128)S(1)} %fusion.4), channel_id=1, replica_groups={{0,1,2,3,4,5,6,7,8,9,10,11,12,13,14,15,16,17,18,19,20,21,22,23,24,25,26..., dimensions={0} | all-to-all | bytes 524288 | tf_op jit(solution)/shard_map/all_to_all | solution.py:19
  40.2 27.5 %all_to_all.32 = f32[16,8,256]{2,1,0:T(8,128)S(1)} all-to-all(f32[16,8,256]{2,1,0:T(8,128)S(1)} %broadcast_in_dim.7), channel_id=1, replica_groups={{0,32,64,96,128,160,192,224,256,288,320,352,384,416,448,480},{8,40,72,1..., dimensions={0} | all-to-all | bytes 262144 | tf_op jit(solution)/shard_map/all_to_all | solution.py:19
  67.7 0.7 broadcast_in_dim.8
  68.5 5.9 %all-to-all-start.4 = ((f32[32,8,256]{2,1,0:T(8,128)}), f32[32,8,256]{2,1,0:T(8,128)S(1)}, u32[]{:S(2)}, u32[]{:S(2)}) async-start(f32[32,8,256]{2,1,0:T(8,128)} %broadcast_in_dim.8), calls=%async_computation.4 | async-start | bytes 524288 | tf_op jit(solution)/shard_map/all_to_all | solution.py:19
  74.4 7.5 %all-to-all-done.4 = f32[32,8,256]{2,1,0:T(8,128)S(1)} async-done(((f32[32,8,256]{2,1,0:T(8,128)}), f32[32,8,256]{2,1,0:T(8,128)S(1)}, u32[]{:S(2)}, u32[]{:S(2)}) %all-to-all-start.4) | async-done | bytes 262176 | tf_op jit(solution)/shard_map/all_to_all | solution.py:19
  81.9 1.1 broadcast_in_dim.6
  82.9 3.7 %all-to-all-start.1 = ((bf16[8,256,256]{2,1,0:T(8,128)(2,1)}), bf16[8,256,256]{2,1,0:T(8,128)(2,1)S(1)}, u32[]{:S(2)}, u32[]{:S(2)}) async-start(bf16[8,256,256]{2,1,0:T(8,128)(2,1)} %broadcast_in_dim.6), calls=%async_computation.1 | async-start | bytes 2097152 | tf_op jit(solution)/shard_map/all_to_all | solution.py:19
  86.7 11.7 %cholesky.50 = f32[128,128]{1,0:T(8,128)S(1)} custom-call(f32[128,128]{1,0:T(8,128)S(1)} %cholesky.118), custom_call_target="Cholesky" | custom-call | tf_op jit(solution)/shard_map/cholesky | solution.py:44
  98.5 9.8 %custom-call.11 = f32[1,128,128]{1,2,0:T(8,128)S(1)} custom-call(f32[1,128,128]{2,1,0:T(8,128)S(1)} %get-tuple-element.23), custom_call_target="InvertDiagBlocksLowerTriangular" | custom-call | tf_op jit(solution)/shard_map/cholesky | solution.py:44
  108.3 0.2 constant_dynamic-update-slice_fusion
  108.5 0.3 convolution_subtract_fusion.1
  108.8 11.7 %cholesky.105 = f32[128,128]{1,0:T(8,128)S(1)} custom-call(f32[128,128]{1,0:T(8,128)S(1)} %convolution_subtract_fusion.1), custom_call_target="Cholesky" | custom-call | tf_op jit(solution)/shard_map/cholesky | solution.py:44
  120.5 0.7 compare_reduce_fusion
  122.6 0.1 triangular_solve.63
  122.7 4.1 %while.1 = (s32[]{:T(128)}, f32[256,256]{1,0:T(8,128)S(1)}, s32[2,2]{1,0:T(2,128)S(1)}, f32[2,128,128]{2,1,0:T(8,128)S(1)}, s32[]{:T(128)}) while((s32[]{:T(128)}, f32[256,256]{1,0:T(8,128)S(1)}, s32[2,2]{1,0:T(2,128)S(1)}, f32[2,128,128]{2,1,0:T(8,128)S(1)}, s32[]{:T(128)}) %tuple.27), condition=%wide.while_cond, body=%wide.while_body.sunk | while | flops 2 | bytes 131181 | solution.py:45
  122.7 0.6 fusion.32
  123.3 1.4 bitcast_dynamic-update-slice_fusion.2
  124.8 0.6 fusion.32
  125.3 1.4 bitcast_dynamic-update-slice_fusion.2
  126.8 19.9 %custom-call.12 = f32[2,128,128]{1,2,0:T(8,128)S(1)} custom-call(f32[2,128,128]{2,1,0:T(8,128)S(1)} %get-tuple-element.9), custom_call_target="InvertDiagBlocksLowerTriangular" | custom-call | tf_op jit(solution)/shard_map/triangular_solve | solution.py:45
  146.7 0.3 fusion.9
  147.0 0.3 convolution_subtract_fusion
  147.2 0.3 fusion.12
  147.6 0.0 all-to-all-done.1
  147.6 0.0 copy-start.1
  147.6 0.5 fusion.2
  148.1 0.5 fusion
  148.5 1.2 copy-done.1
  149.8 1.3 convolution_convert_fusion.1
  151.1 1.0 reshape.39
  152.0 7.0 %all-to-all-start.5 = ((bf16[64,4,1024]{2,1,0:T(4,128)(2,1)}), bf16[64,4,1024]{2,1,0:T(4,128)(2,1)S(1)}, u32[]{:S(2)}, u32[]{:S(2)}) async-start(bf16[64,4,1024]{2,1,0:T(4,128)(2,1)} %reshape.39), calls=%async_computation.5 | async-start | bytes 1048576 | tf_op jit(solution)/shard_map/all_to_all | solution.py:19
  159.1 0.7 constant_dynamic-slice_fusion.1
  159.7 32.7 %all-to-all-done.5 = bf16[64,4,1024]{2,1,0:T(4,128)(2,1)S(1)} async-done(((bf16[64,4,1024]{2,1,0:T(4,128)(2,1)}), bf16[64,4,1024]{2,1,0:T(4,128)(2,1)S(1)}, u32[]{:S(2)}, u32[]{:S(2)}) %all-to-all-start.5) | async-done | bytes 524320 | tf_op jit(solution)/shard_map/all_to_all | solution.py:19
  192.5 0.2 convert_reduce_fusion
  192.7 0.6 broadcast_multiply_fusion
  (13 shorter events, 0.2 us)
Async XLA Ops:
  0.6 1.0 copy-start
  68.5 13.4 %all-to-all-start.4 = ((f32[32,8,256]{2,1,0:T(8,128)}), f32[32,8,256]{2,1,0:T(8,128)S(1)}, u32[]{:S(2)}, u32[]{:S(2)}) async-start(f32[32,8,256]{2,1,0:T(8,128)} %broadcast_in_dim.8), calls=%async_computation.4 | async-start | bytes 524288 | tf_op jit(solution)/shard_map/all_to_all | solution.py:19
  82.9 64.6 %all-to-all-start.1 = ((bf16[8,256,256]{2,1,0:T(8,128)(2,1)}), bf16[8,256,256]{2,1,0:T(8,128)(2,1)S(1)}, u32[]{:S(2)}, u32[]{:S(2)}) async-start(bf16[8,256,256]{2,1,0:T(8,128)(2,1)} %broadcast_in_dim.6), calls=%async_computation.1 | async-start | bytes 2097152 | tf_op jit(solution)/shard_map/all_to_all | solution.py:19
  147.6 2.2 %copy-start.1 = (bf16[2048,1024]{1,0:T(8,128)(2,1)S(1)}, bf16[2048,1024]{1,0:T(8,128)(2,1)}, u32[]{:S(2)}) copy-start(bf16[2048,1024]{1,0:T(8,128)(2,1)} %param.2) | copy-start | bytes 12582916
  152.0 40.4 %all-to-all-start.5 = ((bf16[64,4,1024]{2,1,0:T(4,128)(2,1)}), bf16[64,4,1024]{2,1,0:T(4,128)(2,1)S(1)}, u32[]{:S(2)}, u32[]{:S(2)}) async-start(bf16[64,4,1024]{2,1,0:T(4,128)(2,1)} %reshape.39), calls=%async_computation.5 | async-start | bytes 1048576 | tf_op jit(solution)/shard_map/all_to_all | solution.py:19

commit v2 on v1

v2 whole, which is shorter than its diff:
```python
import functools
import math

import jax
import jax.numpy as jnp
from jax import lax
from jax.experimental import pallas as pl
from jax.experimental.pallas import tpu as pltpu
from jax.sharding import PartitionSpec as P

Y = 4
PANEL, SUB, LANES = 32, 8, 128


def groups(rows, cols):
    depth = rows // Y
    plane = [[(z * Y + y) * cols + c for y in range(Y) for c in range(cols)] for z in range(depth)]
    along_z = [[z * Y + y for z in range(depth)] for y in range(Y)]
    along_y = [[z * Y + y for y in range(Y)] for z in range(depth)]
    return plane, along_y, along_z


def exchange(blocks, axis, members=None):
    return lax.all_to_all(blocks, axis, 0, 0, axis_index_groups=members)


def share(block, count, axis, members=None):
    return exchange(jnp.broadcast_to(block[None], (count,) + block.shape), axis, members)


def factor_kernel(gram_ref, high_ref, low_ref, work, *, scale):
    size = gram_ref.shape[0]
    count, spans = PANEL // SUB, size // LANES
    f32 = jnp.float32
    sub = lax.broadcasted_iota(jnp.int32, (SUB, LANES), 0)
    lanes = lax.broadcasted_iota(jnp.int32, (SUB, LANES), 1)
    work[...] = gram_ref[...]

    def spread(row):
        return jnp.broadcast_to(row, (SUB, LANES))

    def wide(columns):
        return jnp.concatenate([jnp.concatenate([c] * spans, axis=1) for c in columns], axis=0)

    def panel(index, carry):
        start = pl.multiple_of(index * PANEL, PANEL)
        rows = work[pl.ds(start, PANEL), :]
        diagonal = pltpu.roll(rows, (size - start) % size, 1)
        tiles = []
        for g in range(count):
            line = []
            for t in range(spans):
                at = lanes + LANES * t - start
                inside = (at >= 0) & (at < PANEL)
                unit = (at == sub + SUB * g).astype(f32)
                block = rows[SUB * g : SUB * (g + 1), LANES * t : LANES * (t + 1)]
                line.append(jnp.where(inside, unit, block))
            tiles.append(line + [diagonal[SUB * g : SUB * (g + 1), :LANES]])
        inverses, pivots = [], []
        for g in range(count):
            left = range(g, count)
            columns = [
                {h: spread(tiles[h][spans][:, SUB * g + j : SUB * g + j + 1]) for h in left}
                for j in range(SUB)
            ]
            inverse_of, pivot_of = jnp.ones((SUB, LANES), f32), jnp.ones((SUB, LANES), f32)
            for j in range(SUB):
                pivot = spread(columns[j][g][j : j + 1])
                inverse = 1.0 / pivot
                factors = {h: columns[j][h] * inverse for h in left}
                factors[g] = jnp.where(sub > j, factors[g], 0.0)
                for k in range(j + 1, SUB):
                    row = spread(columns[k][g][j : j + 1])
                    for h in left:
                        columns[k][h] = columns[k][h] - factors[h] * row
                for t in range(spans + (g < count - 1)):
                    row = spread(tiles[g][t][j : j + 1])
                    for h in left:
                        tiles[h][t] = tiles[h][t] - factors[h] * row
                inverse_of = jnp.where(sub == j, inverse, inverse_of)
                pivot_of = jnp.where(sub == j, pivot, pivot_of)
            inverses.append(inverse_of)
            pivots.append(pivot_of)
        done = jnp.concatenate([jnp.concatenate(line[:spans], axis=1) for line in tiles], axis=0)
        lane = lax.broadcasted_iota(jnp.int32, (PANEL, size), 1)
        result = done * wide([lax.rsqrt(p) * scale for p in pivots])
        result = jnp.where(lane < start + PANEL, result, 0.0)
        high = result.astype(jnp.bfloat16)
        high_ref[pl.ds(start, PANEL), :] = high
        low_ref[pl.ds(start, PANEL), :] = (result - high.astype(f32)).astype(jnp.bfloat16)
        factors = jnp.where(lane >= start + PANEL, done * wide(inverses), 0.0)
        update = lax.dot_general(
            factors,
            done,
            (((0,), (0,)), ((), ())),
            precision=lax.Precision.HIGHEST,
            preferred_element_type=f32,
        )
        at = lax.broadcasted_iota(jnp.int32, (size, size), 1) - start
        work[...] = jnp.where((at >= 0) & (at < PANEL), 0.0, work[...]) - update
        return carry

    lax.fori_loop(0, size // PANEL, panel, 0)


def inverse_factor(gram, scale):
    pair = jax.ShapeDtypeStruct(gram.shape, jnp.bfloat16)
    return pl.pallas_call(
        functools.partial(factor_kernel, scale=scale),
        out_shape=[pair, pair],
        in_specs=[pl.BlockSpec(memory_space=pltpu.VMEM)],
        out_specs=[pl.BlockSpec(memory_space=pltpu.VMEM)] * 2,
        scratch_shapes=[pltpu.VMEM(gram.shape, jnp.float32)],
        name="inverse_factor",
    )(gram)


def apply_pair(sketch, high, low):
    by_rows = (((1,), (1,)), ((), ()))
    out = lax.dot_general(sketch, high, by_rows, preferred_element_type=jnp.float32)
    out = out + lax.dot_general(sketch, low, by_rows, preferred_element_type=jnp.float32)
    return out.astype(jnp.bfloat16)


def local(activations, start_basis):
    rows, cols = lax.axis_size("row"), lax.axis_size("col")
    rows_dev, rank = activations.shape[0], start_basis.shape[1]
    root_tokens = math.sqrt(rows_dev * rows)
    plane, along_y, along_z = groups(rows, cols)
    plane_size, depth = Y * cols, rows // Y

    partial = jnp.dot(activations, start_basis, preferred_element_type=jnp.float32)
    partial = partial.astype(jnp.bfloat16).reshape(cols, rows_dev // cols, rank)
    own = jnp.sum(exchange(partial, "col").astype(jnp.float32), 0).astype(jnp.bfloat16)
    sketch = share(own, cols, "col").reshape(rows_dev, rank)

    gram = lax.dot_general(own, own, (((0,), (0,)), ((), ())), preferred_element_type=jnp.float32)
    gram = gram.reshape(plane_size, rank // plane_size, rank)
    gram = jnp.sum(exchange(gram, ("row", "col"), plane), 0)
    gram = jnp.sum(share(gram, depth, "row", along_z), 0)
    gram = share(gram, plane_size, ("row", "col"), plane).reshape(rank, rank)

    high, low = inverse_factor(gram, root_tokens)

    def by_y(pair):
        pair = pair.reshape(depth, Y, rank // rows, rank)
        return jnp.swapaxes(pair, 0, 1).reshape(rank, rank)

    turned = apply_pair(sketch, by_y(high), by_y(low))
    projected = lax.dot_general(
        turned, activations, (((0,), (0,)), ((), ())), preferred_element_type=jnp.float32
    )
    projected = projected.astype(jnp.bfloat16).reshape(Y, rank // Y, -1)
    projected = jnp.sum(exchange(projected, "row", along_y).astype(jnp.float32), 0)
    projected = projected.astype(jnp.bfloat16).reshape(depth, rank // rows, -1)
    projected = exchange(projected, "row", along_z).astype(jnp.float32)
    projected = jnp.sum(projected, 0) / root_tokens

    width = rank // cols
    first = lax.axis_index("col") * width
    mine = [lax.dynamic_slice_in_dim(part, first, width, 0) for part in (high, low)]
    return (apply_pair(sketch, *mine), projected)


def solution(mesh):
    return jax.shard_map(
        local,
        mesh=mesh,
        in_specs=(P("row", "col"), P("col", None)),
        out_specs=(P("row", "col"), P("row", "col")),
        check_vma=False,
    )
```

time: 194 us -> 143 us (0.74)
  the two profiles are of different devices: /device:TPU:8 before, /device:TPU:2 now
where the time goes in v2:
time: 143 us; the launch traced here: 142 us
  blocking collectives  75.6 us (53%)
  waiting for transfers between devices  21.6 us (15%)
  matrix products  13.9 us (10%)
  starting transfers between devices  12.7 us (9%)
  Pallas kernels  11.4 us (8%)
  local copies, waits for them, and re-layouts  4.97 us (3%)
    all_to_all x4, blocking collectives, exchange(): return lax.all_to_all(blocks, axis, 0, 0, axis_index_groups=members)  75.6 us
    all_to_all x3, waiting for transfers between devices, exchange(): return lax.all_to_all(blocks, axis, 0, 0, axis_index_groups=members)  21.6 us
    all_to_all x3, starting transfers between devices, exchange(): return lax.all_to_all(blocks, axis, 0, 0, axis_index_groups=members)  12.7 us
    pallas_call x1, Pallas kernels, inverse_factor(): pl.pallas_call(functools.partial(factor_kernel, scale=scale), out_shape=[...  11.4 us
    dot_general x1, matrix products, local(): lax.dot_general(turned, activations, (((0,), (0,)), ((), ())), preferred_...  5.54 us
    dot_general x1, matrix products, local(): jnp.dot(activations, start_basis, preferred_element_type=jnp.float32)  3.44 us
    dot_general x2, matrix products, apply_pair(): lax.dot_general(sketch, high, by_rows, preferred_element_type=jnp.float32)  2.94 us
  transfers between devices with their start and end apart: 3, of which 3 were waited for; matrix products, arithmetic and copies ran while one was open for 4% of the time, Pallas kernels for 8%

profile of v2, /device:TPU:2, one launch (start us, length us, event | category | flops | bytes accessed | tf_op | source)
XLA Modules:
  0.0 142.0 jit_solution(18368777520247641625)
XLA Ops:
  0.6 0.0 copy-start
  0.6 1.0 copy-done
  1.7 3.4 %convolution_convert_fusion = bf16[2048,256]{1,0:T(8,128)(2,1)S(1)} fusion(bf16[2048,1024]{1,0:T(8,128)(2,1)} %param.2, bf16[1024,256]{1,0:T(8,128)(2,1)S(1)} %copy-done), kind=kOutput, calls=%fused_computation.2 | convolution fusion | flops 1074266112 | bytes 5767168 | tf_op jit(solution)/shard_map/dot_general | solution.py:132
  5.1 23.0 %all_to_all.35 = bf16[8,256,256]{2,1,0:T(8,128)(2,1)S(1)} all-to-all(bf16[8,256,256]{2,1,0:T(8,128)(2,1)S(1)} %bitcast.31), channel_id=1, replica_groups=mesh['row'=64,'col'=8] {'col'}, dimensions={0} | all-to-all | bytes 2097152 | tf_op jit(solution)/shard_map/all_to_all | solution.py:24
  28.1 0.1 reduce_sum.51
  28.2 0.1 copy.19
  28.3 0.2 fusion.2
  28.5 11.9 %all_to_all.36 = f32[32,8,256]{2,1,0:T(8,128)S(1)} all-to-all(f32[32,8,256]{2,1,0:T(8,128)S(1)} %fusion.2), channel_id=1, replica_groups={{0,1,2,3,4,5,6,7,8,9,10,11,12,13,14,15,16,17,18,19,20,21,22,23,24,25,26..., dimensions={0} | all-to-all | bytes 524288 | tf_op jit(solution)/shard_map/all_to_all | solution.py:24
  40.5 27.7 %all_to_all.37 = f32[16,8,256]{2,1,0:T(8,128)S(1)} all-to-all(f32[16,8,256]{2,1,0:T(8,128)S(1)} %broadcast_in_dim.7), channel_id=1, replica_groups={{0,32,64,96,128,160,192,224,256,288,320,352,384,416,448,480},{8,40,72,1..., dimensions={0} | all-to-all | bytes 262144 | tf_op jit(solution)/shard_map/all_to_all | solution.py:24
  68.3 13.0 %all_to_all.38 = f32[32,8,256]{2,1,0:T(8,128)} all-to-all(f32[32,8,256]{2,1,0:T(8,128)S(1)} %broadcast_in_dim.8), channel_id=1, replica_groups={{0,1,2,3,4,5,6,7,8,9,10,11,12,13,14,15,16,17,18,19,20,21,22,23,24,25,26..., dimensions={0} | all-to-all | bytes 524288 | tf_op jit(solution)/shard_map/all_to_all | solution.py:24
  81.3 1.1 broadcast_in_dim.6
  82.3 4.9 %all-to-all-start.1 = ((bf16[8,256,256]{2,1,0:T(8,128)(2,1)}), bf16[8,256,256]{2,1,0:T(8,128)(2,1)S(1)}, u32[]{:S(2)}, u32[]{:S(2)}) async-start(bf16[8,256,256]{2,1,0:T(8,128)(2,1)} %broadcast_in_dim.6), calls=%async_computation.1 | async-start | bytes 2097152 | tf_op jit(solution)/shard_map/all_to_all | solution.py:24
  87.3 11.4 %inverse_factor.1 = (bf16[256,256]{1,0:T(8,128)(2,1)}, bf16[256,256]{1,0:T(8,128)(2,1)}) custom-call(f32[256,256]{1,0:T(8,128)} %bitcast.32), custom_call_target="tpu_custom_call" | custom-call | tf_op jit(solution)/shard_map/inverse_factor/pallas_call | solution.py:108
  98.7 0.9 reshape.39
  99.7 0.9 reshape.41
  100.8 1.0 all-to-all-done.1
  101.8 1.8 %fusion.10 = f32[2048,256]{1,0:T(8,128)} fusion(bf16[2048,256]{1,0:T(8,128)(2,1)S(1)} %bitcast.26, bf16[256,256]{1,0:T(8,128)(2,1)S(1)} %reshape.40), kind=kOutput, calls=%fused_computation.18 | convolution fusion | flops 268435456 | bytes 3276800 | tf_op jit(solution)/shard_map/dot_general | solution.py:120
  103.6 5.5 %convolution_convert_fusion.1 = bf16[256,1024]{1,0:T(8,128)(2,1)} fusion(bf16[2048,1024]{1,0:T(8,128)(2,1)} %param.2, f32[2048,256]{1,0:T(8,128)} %fusion.10, bf16[2048,256]{1,0:T(8,128)(2,1)S(1)} %bitcast.27, bf16[256,256]{1,0:T(8,128)(2,1)S(1)} %reshape.42), kind=kOutput, calls=%fused_computation.5 | convolution fusion | flops 1343488000 | bytes 7995392 | tf_op jit(solution)/shard_map/dot_general | solution.py:150
  109.2 3.5 %all-to-all-start.5 = ((bf16[4,64,1024]{2,1,0:T(8,128)(2,1)}), bf16[4,64,1024]{2,1,0:T(8,128)(2,1)S(1)}, u32[]{:S(2)}, u32[]{:S(2)}) async-start(bf16[4,64,1024]{2,1,0:T(8,128)(2,1)} %bitcast.8), calls=%async_computation.5 | async-start | bytes 1048576 | tf_op jit(solution)/shard_map/all_to_all | solution.py:24
  112.6 9.5 %all-to-all-done.5 = bf16[4,64,1024]{2,1,0:T(8,128)(2,1)S(1)} async-done(((bf16[4,64,1024]{2,1,0:T(8,128)(2,1)}), bf16[4,64,1024]{2,1,0:T(8,128)(2,1)S(1)}, u32[]{:S(2)}, u32[]{:S(2)}) %all-to-all-start.5) | async-done | bytes 524320 | tf_op jit(solution)/shard_map/all_to_all | solution.py:24
  122.2 0.1 reduce_sum.54
  122.2 0.7 reshape.44
  122.9 4.4 %all-to-all-start.6 = ((bf16[16,4,1024]{2,1,0:T(4,128)(2,1)}), bf16[16,4,1024]{2,1,0:T(4,128)(2,1)S(1)}, u32[]{:S(2)}, u32[]{:S(2)}) async-start(bf16[16,4,1024]{2,1,0:T(4,128)(2,1)} %reshape.44), calls=%async_computation.6 | async-start | bytes 262144 | tf_op jit(solution)/shard_map/all_to_all | solution.py:24
  127.3 1.1 fusion.6
  128.4 1.8 %fusion.1 = bf16[2048,32]{0,1:T(8,128)(2,1)} fusion(f32[2048,32]{0,1:T(8,128)S(1)} %fusion.6, bf16[2048,256]{1,0:T(8,128)(2,1)S(1)} %bitcast.29, bf16[256,256]{1,0:T(8,128)(2,1)} %get-tuple-element.5, s32[]{:T(128)S(6)} %select_n.4), kind=kOutput, calls=%fused_computation.4 | convolution fusion | flops 33685504 | bytes 1458180 | tf_op jit(solution)/shard_map/dot_general | solution.py:121
  130.3 11.0 %all-to-all-done.6 = bf16[16,4,1024]{2,1,0:T(4,128)(2,1)S(1)} async-done(((bf16[16,4,1024]{2,1,0:T(4,128)(2,1)}), bf16[16,4,1024]{2,1,0:T(4,128)(2,1)S(1)}, u32[]{:S(2)}, u32[]{:S(2)}) %all-to-all-start.6) | async-done | bytes 131104 | tf_op jit(solution)/shard_map/all_to_all | solution.py:24
  141.3 0.1 convert_reduce_fusion
  141.3 0.6 broadcast_multiply_fusion
  (8 shorter events, 0.3 us)
Async XLA Ops:
  0.6 1.0 copy-start
  82.3 19.4 %all-to-all-start.1 = ((bf16[8,256,256]{2,1,0:T(8,128)(2,1)}), bf16[8,256,256]{2,1,0:T(8,128)(2,1)S(1)}, u32[]{:S(2)}, u32[]{:S(2)}) async-start(bf16[8,256,256]{2,1,0:T(8,128)(2,1)} %broadcast_in_dim.6), calls=%async_computation.1 | async-start | bytes 2097152 | tf_op jit(solution)/shard_map/all_to_all | solution.py:24
  109.2 13.0 %all-to-all-start.5 = ((bf16[4,64,1024]{2,1,0:T(8,128)(2,1)}), bf16[4,64,1024]{2,1,0:T(8,128)(2,1)S(1)}, u32[]{:S(2)}, u32[]{:S(2)}) async-start(bf16[4,64,1024]{2,1,0:T(8,128)(2,1)} %bitcast.8), calls=%async_computation.5 | async-start | bytes 1048576 | tf_op jit(solution)/shard_map/all_to_all | solution.py:24
  122.9 18.3 %all-to-all-start.6 = ((bf16[16,4,1024]{2,1,0:T(4,128)(2,1)}), bf16[16,4,1024]{2,1,0:T(4,128)(2,1)S(1)}, u32[]{:S(2)}, u32[]{:S(2)}) async-start(bf16[16,4,1024]{2,1,0:T(4,128)(2,1)} %reshape.44), calls=%async_computation.6 | async-start | bytes 262144 | tf_op jit(solution)/shard_map/all_to_all | solution.py:24

commit v3 on v2

--- a/solution.py
+++ b/solution.py
@@ -9,7 +9,7 @@
 from jax.sharding import PartitionSpec as P
 
 Y = 4
-PANEL, SUB, LANES = 32, 8, 128
+PANEL, SUB, LANES = 64, 8, 128
 
 
 def groups(rows, cols):
@@ -115,6 +115,33 @@
     )(gram)
 
 
+def project_kernel(sketch_ref, high_ref, low_ref, activations_ref, out_ref, *, depth, lines):
+    rank = high_ref.shape[0]
+    f32, bf16 = jnp.float32, jnp.bfloat16
+    to = lax.broadcasted_iota(jnp.int32, (rank, rank), 0)
+    source = lax.broadcasted_iota(jnp.int32, (rank, rank), 1)
+    y, z, line = to // (depth * lines), to // lines % depth, to % lines
+    turn = (source == (z * Y + y) * lines + line).astype(bf16)
+    by_rows = (((1,), (1,)), ((), ()))
+    basis = jnp.zeros((rank, sketch_ref.shape[0]), f32)
+    for part in (high_ref, low_ref):
+        turned = jnp.dot(turn, part[...], preferred_element_type=f32).astype(bf16)
+        basis += lax.dot_general(turned, sketch_ref[...], by_rows, preferred_element_type=f32)
+    basis = basis.astype(bf16)
+    out_ref[...] = jnp.dot(basis, activations_ref[...], preferred_element_type=f32).astype(bf16)
+
+
+def project(sketch, high, low, activations, depth, lines):
+    return pl.pallas_call(
+        functools.partial(project_kernel, depth=depth, lines=lines),
+        out_shape=jax.ShapeDtypeStruct((high.shape[0], activations.shape[1]), jnp.bfloat16),
+        in_specs=[pl.BlockSpec(memory_space=pltpu.VMEM)] * 4,
+        out_specs=pl.BlockSpec(memory_space=pltpu.VMEM),
+        compiler_params=pltpu.CompilerParams(vmem_limit_bytes=32 * 2**20),
+        name="project",
+    )(sketch, high, low, activations)
+
+
 def apply_pair(sketch, high, low):
     by_rows = (((1,), (1,)), ((), ()))
     out = lax.dot_general(sketch, high, by_rows, preferred_element_type=jnp.float32)
@@ -142,15 +169,7 @@
 
     high, low = inverse_factor(gram, root_tokens)
 
-    def by_y(pair):
-        pair = pair.reshape(depth, Y, rank // rows, rank)
-        return jnp.swapaxes(pair, 0, 1).reshape(rank, rank)
-
-    turned = apply_pair(sketch, by_y(high), by_y(low))
-    projected = lax.dot_general(
-        turned, activations, (((0,), (0,)), ((), ())), preferred_element_type=jnp.float32
-    )
-    projected = projected.astype(jnp.bfloat16).reshape(Y, rank // Y, -1)
+    projected = project(sketch, high, low, activations, depth, rank // rows).reshape(Y, rank // Y, -1)
     projected = jnp.sum(exchange(projected, "row", along_y).astype(jnp.float32), 0)
     projected = projected.astype(jnp.bfloat16).reshape(depth, rank // rows, -1)
     projected = exchange(projected, "row", along_z).astype(jnp.float32)

time: 143 us -> 142 us (level)
  matrix products: 13.9 us -> 6.56 us
  waiting for transfers between devices: 21.6 us -> 24.8 us
  local copies, waits for them, and re-layouts: 4.97 us -> 6.92 us
  Pallas kernels: 11.4 us -> 13 us
    dot_general x1 -> x0, matrix products: 5.54 us -> none  [local(): lax.dot_general(turned, activations, (((0,), (0,)), ((), ())), preferred_...]
    unnamed x2 -> x8, local copies, waits for them, and re-layouts: 1.04 us -> 5.04 us
    all_to_all x3, waiting for transfers between devices: 21.6 us -> 24.8 us  [exchange(): return lax.all_to_all(blocks, axis, 0, 0, axis_index_groups=members)]
    pallas_call x0 -> x1, Pallas kernels: none -> 2.7 us  [project(): pl.pallas_call(functools.partial(project_kernel, depth=depth, lines=lines...]
    reshape x6 -> x0, local copies, waits for them, and re-layouts: 2.05 us -> none  [the longest x4 1.98 us: by_y(): pair = pair.reshape(depth, Y, rank // rows, rank)]
    dot_general x2 -> x1, matrix products: 2.94 us -> 1.13 us  [apply_pair(): lax.dot_general(sketch, high, by_rows, preferred_element_type=jnp.float32)]
  transfers between devices with their start and end apart: 3 -> 3, of which waited for: 3 -> 3; matrix products, arithmetic and copies ran while one was open for 4% -> 2% of each run, Pallas kernels for 8% -> 7%
where the time goes in v3:
time: 142 us; the launch traced here: 141 us
  blocking collectives  75.6 us (53%)
  waiting for transfers between devices  24.8 us (17%)
  Pallas kernels  13 us (9%)
  starting transfers between devices  12.7 us (9%)
  local copies, waits for them, and re-layouts  6.92 us (5%)
  matrix products  6.56 us (5%)
    all_to_all x4, blocking collectives, exchange(): return lax.all_to_all(blocks, axis, 0, 0, axis_index_groups=members)  75.6 us
    all_to_all x3, waiting for transfers between devices, exchange(): return lax.all_to_all(blocks, axis, 0, 0, axis_index_groups=members)  24.8 us
    all_to_all x3, starting transfers between devices, exchange(): return lax.all_to_all(blocks, axis, 0, 0, axis_index_groups=members)  12.7 us
    pallas_call x1, Pallas kernels, inverse_factor(): pl.pallas_call(functools.partial(factor_kernel, scale=scale), out_shape=[...  10.3 us
    unnamed x8, local copies, waits for them, and re-layouts  5.04 us
    dot_general x1, matrix products, local(): jnp.dot(activations, start_basis, preferred_element_type=jnp.float32)  3.44 us
  transfers between devices with their start and end apart: 3, of which 3 were waited for; matrix products, arithmetic and copies ran while one was open for 2% of the time, Pallas kernels for 7%

profile of v3, /device:TPU:2, one launch (start us, length us, event | category | flops | bytes accessed | tf_op | source)
XLA Modules:
  0.0 141.3 jit_solution(13122200870021777820)
XLA Ops:
  0.6 0.0 copy-start
  0.6 1.0 copy-done
  1.7 3.4 %convolution_convert_fusion = bf16[2048,256]{1,0:T(8,128)(2,1)S(1)} fusion(bf16[2048,1024]{1,0:T(8,128)(2,1)} %activations_ref.1, bf16[1024,256]{1,0:T(8,128)(2,1)S(1)} %copy-done), kind=kOutput, calls=%fused_computation | convolution fusion | flops 1074266112 | bytes 5767168 | tf_op jit(solution)/shard_map/dot_general | solution.py:159
  5.1 23.0 %all_to_all.35 = bf16[8,256,256]{2,1,0:T(8,128)(2,1)S(1)} all-to-all(bf16[8,256,256]{2,1,0:T(8,128)(2,1)S(1)} %bitcast.19), channel_id=1, replica_groups=mesh['row'=64,'col'=8] {'col'}, dimensions={0} | all-to-all | bytes 2097152 | tf_op jit(solution)/shard_map/all_to_all | solution.py:24
  28.1 0.1 reduce_sum.51
  28.2 0.1 copy.10
  28.3 0.2 fusion.1
  28.5 11.9 %all_to_all.36 = f32[32,8,256]{2,1,0:T(8,128)S(1)} all-to-all(f32[32,8,256]{2,1,0:T(8,128)S(1)} %fusion.1), channel_id=1, replica_groups={{0,1,2,3,4,5,6,7,8,9,10,11,12,13,14,15,16,17,18,19,20,21,22,23,24,25,26..., dimensions={0} | all-to-all | bytes 524288 | tf_op jit(solution)/shard_map/all_to_all | solution.py:24
  40.5 27.7 %all_to_all.37 = f32[16,8,256]{2,1,0:T(8,128)S(1)} all-to-all(f32[16,8,256]{2,1,0:T(8,128)S(1)} %broadcast_in_dim.7), channel_id=1, replica_groups={{0,32,64,96,128,160,192,224,256,288,320,352,384,416,448,480},{8,40,72,1..., dimensions={0} | all-to-all | bytes 262144 | tf_op jit(solution)/shard_map/all_to_all | solution.py:24
  68.3 13.0 %all_to_all.38 = f32[32,8,256]{2,1,0:T(8,128)} all-to-all(f32[32,8,256]{2,1,0:T(8,128)S(1)} %broadcast_in_dim.8), channel_id=1, replica_groups={{0,1,2,3,4,5,6,7,8,9,10,11,12,13,14,15,16,17,18,19,20,21,22,23,24,25,26..., dimensions={0} | all-to-all | bytes 524288 | tf_op jit(solution)/shard_map/all_to_all | solution.py:24
  81.3 1.1 broadcast_in_dim.6
  82.3 4.9 %all-to-all-start.1 = ((bf16[8,256,256]{2,1,0:T(8,128)(2,1)}), bf16[8,256,256]{2,1,0:T(8,128)(2,1)S(1)}, u32[]{:S(2)}, u32[]{:S(2)}) async-start(bf16[8,256,256]{2,1,0:T(8,128)(2,1)} %broadcast_in_dim.6), calls=%async_computation.1 | async-start | bytes 2097152 | tf_op jit(solution)/shard_map/all_to_all | solution.py:24
  87.3 10.3 %inverse_factor.1 = (bf16[256,256]{1,0:T(8,128)(2,1)}, bf16[256,256]{1,0:T(8,128)(2,1)}) custom-call(f32[256,256]{1,0:T(8,128)} %bitcast.20), custom_call_target="tpu_custom_call" | custom-call | tf_op jit(solution)/shard_map/inverse_factor/pallas_call | solution.py:108
  97.5 4.3 %all-to-all-done.1 = bf16[8,256,256]{2,1,0:T(8,128)(2,1)S(1)} async-done(((bf16[8,256,256]{2,1,0:T(8,128)(2,1)}), bf16[8,256,256]{2,1,0:T(8,128)(2,1)S(1)}, u32[]{:S(2)}, u32[]{:S(2)}) %all-to-all-start.1) | async-done | bytes 1048608 | tf_op jit(solution)/shard_map/all_to_all | solution.py:24
  101.8 0.0 copy-start.1
  101.8 2.2 %copy-done.1 = bf16[2048,1024]{1,0:T(8,128)(2,1)S(1)} copy-done((bf16[2048,1024]{1,0:T(8,128)(2,1)S(1)}, bf16[2048,1024]{1,0:T(8,128)(2,1)}, u32[]{:S(2)}) %copy-start.1) | copy-done | bytes 4194328
  104.0 0.0 copy-start.2
  104.0 0.9 copy-done.2
  104.9 0.0 copy-start.3
  104.9 0.9 copy-done.3
  105.8 2.7 %project.1 = bf16[256,1024]{1,0:T(8,128)(2,1)} custom-call(bf16[2048,256]{1,0:T(8,128)(2,1)S(1)} %bitcast.15, bf16[256,256]{1,0:T(8,128)(2,1)S(1)} %copy-done.3, bf16[256,256]{1,0:T(8,128)(2,1)S(1)} %copy-done.2, bf16[2048,1024]{1,0:T(8,128)(2,1)S(1)} %copy-done.1), custom_call_target="tpu_custom_call" | custom-call | tf_op jit(solution)/shard_map/project/pallas_call | solution.py:135
  108.5 3.5 %all-to-all-start.5 = ((bf16[4,64,1024]{2,1,0:T(8,128)(2,1)}), bf16[4,64,1024]{2,1,0:T(8,128)(2,1)S(1)}, u32[]{:S(2)}, u32[]{:S(2)}) async-start(bf16[4,64,1024]{2,1,0:T(8,128)(2,1)} %bitcast.6), calls=%async_computation.5 | async-start | bytes 1048576 | tf_op jit(solution)/shard_map/all_to_all | solution.py:24
  112.0 9.5 %all-to-all-done.5 = bf16[4,64,1024]{2,1,0:T(8,128)(2,1)S(1)} async-done(((bf16[4,64,1024]{2,1,0:T(8,128)(2,1)}), bf16[4,64,1024]{2,1,0:T(8,128)(2,1)S(1)}, u32[]{:S(2)}, u32[]{:S(2)}) %all-to-all-start.5) | async-done | bytes 524320 | tf_op jit(solution)/shard_map/all_to_all | solution.py:24
  121.5 0.1 reduce_sum.54
  121.6 0.7 reshape.28
  122.3 4.4 %all-to-all-start.6 = ((bf16[16,4,1024]{2,1,0:T(4,128)(2,1)}), bf16[16,4,1024]{2,1,0:T(4,128)(2,1)S(1)}, u32[]{:S(2)}, u32[]{:S(2)}) async-start(bf16[16,4,1024]{2,1,0:T(4,128)(2,1)} %reshape.28), calls=%async_computation.6 | async-start | bytes 262144 | tf_op jit(solution)/shard_map/all_to_all | solution.py:24
  126.7 1.1 fusion.5
  127.8 1.8 %fusion = bf16[2048,32]{0,1:T(8,128)(2,1)} fusion(f32[2048,32]{0,1:T(8,128)S(1)} %fusion.5, bf16[2048,256]{1,0:T(8,128)(2,1)S(1)} %bitcast.17, bf16[256,256]{1,0:T(8,128)(2,1)} %get-tuple-element.5.low_ref, s32[]{:T(128)S(6)} %select_n.4), kind=kOutput, calls=%fused_computation.2 | convolution fusion | flops 33685504 | bytes 1458180 | tf_op jit(solution)/shard_map/dot_general | solution.py:148
  129.6 11.0 %all-to-all-done.6 = bf16[16,4,1024]{2,1,0:T(4,128)(2,1)S(1)} async-done(((bf16[16,4,1024]{2,1,0:T(4,128)(2,1)}), bf16[16,4,1024]{2,1,0:T(4,128)(2,1)S(1)}, u32[]{:S(2)}, u32[]{:S(2)}) %all-to-all-start.6) | async-done | bytes 131104 | tf_op jit(solution)/shard_map/all_to_all | solution.py:24
  140.6 0.1 convert_reduce_fusion
  140.7 0.6 broadcast_multiply_fusion
  (4 shorter events, 0.1 us)
Async XLA Ops:
  0.6 1.0 copy-start
  82.3 19.4 %all-to-all-start.1 = ((bf16[8,256,256]{2,1,0:T(8,128)(2,1)}), bf16[8,256,256]{2,1,0:T(8,128)(2,1)S(1)}, u32[]{:S(2)}, u32[]{:S(2)}) async-start(bf16[8,256,256]{2,1,0:T(8,128)(2,1)} %broadcast_in_dim.6), calls=%async_computation.1 | async-start | bytes 2097152 | tf_op jit(solution)/shard_map/all_to_all | solution.py:24
  101.8 2.2 %copy-start.1 = (bf16[2048,1024]{1,0:T(8,128)(2,1)S(1)}, bf16[2048,1024]{1,0:T(8,128)(2,1)}, u32[]{:S(2)}) copy-start(bf16[2048,1024]{1,0:T(8,128)(2,1)} %activations_ref.1) | copy-start | bytes 12582916
  104.0 0.9 copy-start.2
  104.9 0.9 copy-start.3
  108.5 13.0 %all-to-all-start.5 = ((bf16[4,64,1024]{2,1,0:T(8,128)(2,1)}), bf16[4,64,1024]{2,1,0:T(8,128)(2,1)S(1)}, u32[]{:S(2)}, u32[]{:S(2)}) async-start(bf16[4,64,1024]{2,1,0:T(8,128)(2,1)} %bitcast.6), calls=%async_computation.5 | async-start | bytes 1048576 | tf_op jit(solution)/shard_map/all_to_all | solution.py:24
  122.3 18.3 %all-to-all-start.6 = ((bf16[16,4,1024]{2,1,0:T(4,128)(2,1)}), bf16[16,4,1024]{2,1,0:T(4,128)(2,1)S(1)}, u32[]{:S(2)}, u32[]{:S(2)}) async-start(bf16[16,4,1024]{2,1,0:T(4,128)(2,1)} %reshape.28), calls=%async_computation.6 | async-start | bytes 262144 | tf_op jit(solution)/shard_map/all_to_all | solution.py:24

commit v4 on v3

--- a/solution.py
+++ b/solution.py
@@ -10,6 +10,7 @@
 
 Y = 4
 PANEL, SUB, LANES = 64, 8, 128
+VMEM_BYTES = 58 * 2**20
 
 
 def groups(rows, cols):
@@ -28,7 +29,7 @@
     return exchange(jnp.broadcast_to(block[None], (count,) + block.shape), axis, members)
 
 
-def factor_kernel(gram_ref, high_ref, low_ref, work, *, scale):
+def invert_factor(gram_ref, out_ref, work, scale):
     size = gram_ref.shape[0]
     count, spans = PANEL // SUB, size // LANES
     f32 = jnp.float32
@@ -84,10 +85,7 @@
         done = jnp.concatenate([jnp.concatenate(line[:spans], axis=1) for line in tiles], axis=0)
         lane = lax.broadcasted_iota(jnp.int32, (PANEL, size), 1)
         result = done * wide([lax.rsqrt(p) * scale for p in pivots])
-        result = jnp.where(lane < start + PANEL, result, 0.0)
-        high = result.astype(jnp.bfloat16)
-        high_ref[pl.ds(start, PANEL), :] = high
-        low_ref[pl.ds(start, PANEL), :] = (result - high.astype(f32)).astype(jnp.bfloat16)
+        out_ref[pl.ds(start, PANEL), :] = jnp.where(lane < start + PANEL, result, 0.0)
         factors = jnp.where(lane >= start + PANEL, done * wide(inverses), 0.0)
         update = lax.dot_general(
             factors,
@@ -103,43 +101,59 @@
     lax.fori_loop(0, size // PANEL, panel, 0)
 
 
-def inverse_factor(gram, scale):
-    pair = jax.ShapeDtypeStruct(gram.shape, jnp.bfloat16)
-    return pl.pallas_call(
-        functools.partial(factor_kernel, scale=scale),
-        out_shape=[pair, pair],
-        in_specs=[pl.BlockSpec(memory_space=pltpu.VMEM)],
-        out_specs=[pl.BlockSpec(memory_space=pltpu.VMEM)] * 2,
-        scratch_shapes=[pltpu.VMEM(gram.shape, jnp.float32)],
-        name="inverse_factor",
-    )(gram)
-
-
-def project_kernel(sketch_ref, high_ref, low_ref, activations_ref, out_ref, *, depth, lines):
-    rank = high_ref.shape[0]
+def split(matrix):
+    high = matrix.astype(jnp.bfloat16)
+    return high, (matrix - high.astype(jnp.float32)).astype(jnp.bfloat16)
+
+
+def project_kernel(
+    gram_ref, sketch_hbm, activations_hbm, inverse_ref, out_ref,
+    work, sketch_ref, activations_ref, done, *, scale, depth, lines,
+):
+    fetches = [
+        pltpu.make_async_copy(sketch_hbm, sketch_ref, done.at[0]),
+        pltpu.make_async_copy(activations_hbm, activations_ref, done.at[1]),
+    ]
+    for fetch in fetches:
+        fetch.start()
+    invert_factor(gram_ref, inverse_ref, work, scale)
+    rank = gram_ref.shape[0]
     f32, bf16 = jnp.float32, jnp.bfloat16
     to = lax.broadcasted_iota(jnp.int32, (rank, rank), 0)
     source = lax.broadcasted_iota(jnp.int32, (rank, rank), 1)
     y, z, line = to // (depth * lines), to // lines % depth, to % lines
     turn = (source == (z * Y + y) * lines + line).astype(bf16)
     by_rows = (((1,), (1,)), ((), ()))
-    basis = jnp.zeros((rank, sketch_ref.shape[0]), f32)
-    for part in (high_ref, low_ref):
-        turned = jnp.dot(turn, part[...], preferred_element_type=f32).astype(bf16)
-        basis += lax.dot_general(turned, sketch_ref[...], by_rows, preferred_element_type=f32)
-    basis = basis.astype(bf16)
+    turned = [
+        jnp.dot(turn, part, preferred_element_type=f32).astype(bf16)
+        for part in split(inverse_ref[...])
+    ]
+    fetches[0].wait()
+    basis = sum(
+        lax.dot_general(part, sketch_ref[...], by_rows, preferred_element_type=f32)
+        for part in turned
+    ).astype(bf16)
+    fetches[1].wait()
     out_ref[...] = jnp.dot(basis, activations_ref[...], preferred_element_type=f32).astype(bf16)
 
 
-def project(sketch, high, low, activations, depth, lines):
+def project(gram, sketch, activations, scale, depth, lines):
+    in_vmem, in_hbm = pl.BlockSpec(memory_space=pltpu.VMEM), pl.BlockSpec(memory_space=pltpu.HBM)
+    out = jax.ShapeDtypeStruct((gram.shape[0], activations.shape[1]), jnp.bfloat16)
     return pl.pallas_call(
-        functools.partial(project_kernel, depth=depth, lines=lines),
-        out_shape=jax.ShapeDtypeStruct((high.shape[0], activations.shape[1]), jnp.bfloat16),
-        in_specs=[pl.BlockSpec(memory_space=pltpu.VMEM)] * 4,
-        out_specs=pl.BlockSpec(memory_space=pltpu.VMEM),
-        compiler_params=pltpu.CompilerParams(vmem_limit_bytes=32 * 2**20),
+        functools.partial(project_kernel, scale=scale, depth=depth, lines=lines),
+        out_shape=[gram, out],
+        in_specs=[in_vmem, in_hbm, in_hbm],
+        out_specs=[in_vmem, in_vmem],
+        scratch_shapes=[
+            pltpu.VMEM(gram.shape, jnp.float32),
+            pltpu.VMEM(sketch.shape, jnp.bfloat16),
+            pltpu.VMEM(activations.shape, jnp.bfloat16),
+            pltpu.SemaphoreType.DMA((2,)),
+        ],
+        compiler_params=pltpu.CompilerParams(vmem_limit_bytes=VMEM_BYTES),
         name="project",
-    )(sketch, high, low, activations)
+    )(gram, sketch, activations)
 
 
 def apply_pair(sketch, high, low):
@@ -158,8 +172,10 @@
 
     partial = jnp.dot(activations, start_basis, preferred_element_type=jnp.float32)
     partial = partial.astype(jnp.bfloat16).reshape(cols, rows_dev // cols, rank)
-    own = jnp.sum(exchange(partial, "col").astype(jnp.float32), 0).astype(jnp.bfloat16)
-    sketch = share(own, cols, "col").reshape(rows_dev, rank)
+    parts = exchange(partial, "col")
+    own = jnp.sum(parts.astype(jnp.float32), 0).astype(jnp.bfloat16)
+    sent = jnp.sum(lax.optimization_barrier(parts).astype(jnp.float32), 0).astype(jnp.bfloat16)
+    sketch = lax.all_gather(sent, "col", axis=0, tiled=True)
 
     gram = lax.dot_general(own, own, (((0,), (0,)), ((), ())), preferred_element_type=jnp.float32)
     gram = gram.reshape(plane_size, rank // plane_size, rank)
@@ -167,17 +183,17 @@
     gram = jnp.sum(share(gram, depth, "row", along_z), 0)
     gram = share(gram, plane_size, ("row", "col"), plane).reshape(rank, rank)
 
-    high, low = inverse_factor(gram, root_tokens)
-
-    projected = project(sketch, high, low, activations, depth, rank // rows).reshape(Y, rank // Y, -1)
+    lines = rank // rows
+    inverse, projected = project(gram, sketch, activations, root_tokens, depth, lines)
+    projected = projected.reshape(Y, rank // Y, -1)
     projected = jnp.sum(exchange(projected, "row", along_y).astype(jnp.float32), 0)
-    projected = projected.astype(jnp.bfloat16).reshape(depth, rank // rows, -1)
+    projected = projected.astype(jnp.bfloat16).reshape(depth, lines, -1)
     projected = exchange(projected, "row", along_z).astype(jnp.float32)
     projected = jnp.sum(projected, 0) / root_tokens
 
     width = rank // cols
     first = lax.axis_index("col") * width
-    mine = [lax.dynamic_slice_in_dim(part, first, width, 0) for part in (high, low)]
+    mine = split(lax.dynamic_slice_in_dim(inverse, first, width, 0))
     return (apply_pair(sketch, *mine), projected)
 
 

time: 142 us -> 143 us (level)
  the two profiles are of different devices: /device:TPU:2 before, /device:TPU:32 now
where the time goes in v4:
time: 143 us
  blocking collectives  76.1 us (53%)
  waiting for transfers between devices  20.9 us (15%)
  between operations  14.1 us (10%)
  Pallas kernels  13.1 us (9%)
  starting transfers between devices  8.36 us (6%)
  matrix products  6.64 us (5%)
  local copies, waits for them, and re-layouts  1.83 us (1%)
  other arithmetic  1.79 us (1%)
    all_to_all x4, blocking collectives, exchange(): return lax.all_to_all(blocks, axis, 0, 0, axis_index_groups=members)  76.1 us
    all_to_all x2, waiting for transfers between devices, exchange(): return lax.all_to_all(blocks, axis, 0, 0, axis_index_groups=members)  20.8 us
    pallas_call x1, Pallas kernels, project(): pl.pallas_call(functools.partial(project_kernel, scale=scale, depth=depth...  13.1 us
    all_to_all x2, starting transfers between devices, exchange(): return lax.all_to_all(blocks, axis, 0, 0, axis_index_groups=members)  8.32 us
    dot_general x1, matrix products, local(): jnp.dot(activations, start_basis, preferred_element_type=jnp.float32)  3.44 us
  transfers between devices with their start and end apart: 3, of which 2 were waited for; matrix products, arithmetic and copies ran while one was open for 2% of the time, Pallas kernels for 0%

profile of v4, /device:TPU:32, one launch (start us, length us, event | category | flops | bytes accessed | tf_op | source)
XLA Modules:
  0.0 142.8 jit_solution(11279298556519636528)
XLA Ops:
  7.2 0.0 copy-start
  7.2 0.0 all-gather.2.cloned.1.call-start
  7.2 1.0 copy-done
  8.2 3.4 %convolution_convert_fusion = bf16[2048,256]{1,0:T(8,128)(2,1)S(1)} fusion(bf16[2048,1024]{1,0:T(8,128)(2,1)} %activations_hbm.1, bf16[1024,256]{1,0:T(8,128)(2,1)S(1)} %copy-done), kind=kOutput, calls=%fused_computation | convolution fusion | flops 1074266112 | bytes 5767168 | tf_op jit(solution)/shard_map/dot_general | solution.py:173
  11.7 20.2 %all_to_all.30 = bf16[8,256,256]{2,1,0:T(8,128)(2,1)S(1)} all-to-all(bf16[8,256,256]{2,1,0:T(8,128)(2,1)S(1)} %bitcast.15), channel_id=1, replica_groups=mesh['row'=64,'col'=8] {'col'}, dimensions={0} | all-to-all | bytes 2097152 | tf_op jit(solution)/shard_map/all_to_all | solution.py:25
  31.9 0.8 reduce_sum.63
  32.7 0.0 all-gather.2.cloned.1.call-update
  32.7 0.1 reduce_sum.64
  32.8 0.1 copy.10
  33.0 0.2 fusion.1
  33.1 14.2 %all_to_all.31 = f32[32,8,256]{2,1,0:T(8,128)S(1)} all-to-all(f32[32,8,256]{2,1,0:T(8,128)S(1)} %fusion.1), channel_id=1, replica_groups={{0,1,2,3,4,5,6,7,8,9,10,11,12,13,14,15,16,17,18,19,20,21,22,23,24,25,26..., dimensions={0} | all-to-all | bytes 524288 | tf_op jit(solution)/shard_map/all_to_all | solution.py:25
  47.4 28.9 %all_to_all.32 = f32[16,8,256]{2,1,0:T(8,128)S(1)} all-to-all(f32[16,8,256]{2,1,0:T(8,128)S(1)} %broadcast_in_dim.4), channel_id=1, replica_groups={{0,32,64,96,128,160,192,224,256,288,320,352,384,416,448,480},{8,40,72,1..., dimensions={0} | all-to-all | bytes 262144 | tf_op jit(solution)/shard_map/all_to_all | solution.py:25
  76.3 12.8 %all_to_all.33 = f32[32,8,256]{2,1,0:T(8,128)} all-to-all(f32[32,8,256]{2,1,0:T(8,128)S(1)} %broadcast_in_dim.5), channel_id=1, replica_groups={{0,1,2,3,4,5,6,7,8,9,10,11,12,13,14,15,16,17,18,19,20,21,22,23,24,25,26..., dimensions={0} | all-to-all | bytes 524288 | tf_op jit(solution)/shard_map/all_to_all | solution.py:25
  89.1 0.0 all-gather.2.cloned.1.call-done.sketch_hbm
  89.1 0.0 copy-start.1
  89.1 13.1 %project.1 = (f32[256,256]{1,0:T(8,128)}, bf16[256,1024]{1,0:T(8,128)(2,1)}) custom-call(f32[256,256]{1,0:T(8,128)} %bitcast.16, bf16[2048,256]{1,0:T(8,128)(2,1)} %all-gather.2.cloned.1.call-done.sketch_hbm, bf16[2048,1024]{1,0:T(8,128)(2,1)} %activations_hbm.1), custom_call_target="tpu_custom_call" | custom-call | tf_op jit(solution)/shard_map/project/pallas_call | solution.py:143
  102.3 3.5 %all-to-all-start.4 = ((bf16[4,64,1024]{2,1,0:T(8,128)(2,1)}), bf16[4,64,1024]{2,1,0:T(8,128)(2,1)S(1)}, u32[]{:S(2)}, u32[]{:S(2)}) async-start(bf16[4,64,1024]{2,1,0:T(8,128)(2,1)} %bitcast.17), calls=%async_computation.4 | async-start | bytes 1048576 | tf_op jit(solution)/shard_map/all_to_all | solution.py:25
  105.8 10.2 %all-to-all-done.4 = bf16[4,64,1024]{2,1,0:T(8,128)(2,1)S(1)} async-done(((bf16[4,64,1024]{2,1,0:T(8,128)(2,1)}), bf16[4,64,1024]{2,1,0:T(8,128)(2,1)S(1)}, u32[]{:S(2)}, u32[]{:S(2)}) %all-to-all-start.4) | async-done | bytes 524320 | tf_op jit(solution)/shard_map/all_to_all | solution.py:25
  115.9 0.1 reduce_sum.67
  116.0 0.7 reshape.23
  116.7 4.8 %all-to-all-start.5 = ((bf16[16,4,1024]{2,1,0:T(4,128)(2,1)}), bf16[16,4,1024]{2,1,0:T(4,128)(2,1)S(1)}, u32[]{:S(2)}, u32[]{:S(2)}) async-start(bf16[16,4,1024]{2,1,0:T(4,128)(2,1)} %reshape.23), calls=%async_computation.5 | async-start | bytes 262144 | tf_op jit(solution)/shard_map/all_to_all | solution.py:25
  121.5 0.0 copy-done.1
  121.5 1.2 fusion.4
  122.7 1.8 %fusion = bf16[2048,32]{0,1:T(8,128)(2,1)} fusion(f32[2048,32]{0,1:T(8,128)S(1)} %fusion.4, bf16[2048,256]{1,0:T(8,128)(2,1)S(1)} %copy-done.1, f32[256,256]{1,0:T(8,128)} %get-tuple-element.4, s32[]{:T(128)S(6)} %select_n.3), kind=kOutput, calls=%fused_computation.2 | convolution fusion | flops 33718272 | bytes 1474564 | tf_op jit(solution)/shard_map/dot_general | solution.py:162
  124.6 10.7 %all-to-all-done.5 = bf16[16,4,1024]{2,1,0:T(4,128)(2,1)S(1)} async-done(((bf16[16,4,1024]{2,1,0:T(4,128)(2,1)}), bf16[16,4,1024]{2,1,0:T(4,128)(2,1)S(1)}, u32[]{:S(2)}, u32[]{:S(2)}) %all-to-all-start.5) | async-done | bytes 131104 | tf_op jit(solution)/shard_map/all_to_all | solution.py:25
  135.2 0.1 convert_reduce_fusion
  135.3 0.6 broadcast_multiply_fusion
  (4 shorter events, 0.1 us)
Async XLA Ops:
  7.2 1.0 copy-start
  7.2 81.9 %all-gather.2.cloned.1.call-start = ((), (), s32[]{:S(2)}) async-start(), calls=%async_computation.6 | async-start | bytes 1179648 | tf_op jit(solution)/shard_map/all_gather | solution.py:178
  89.1 32.4 %copy-start.1 = (bf16[2048,256]{1,0:T(8,128)(2,1)S(1)}, bf16[2048,256]{1,0:T(8,128)(2,1)}, u32[]{:S(2)}) copy-start(bf16[2048,256]{1,0:T(8,128)(2,1)} %all-gather.2.cloned.1.call-done.sketch_hbm) | copy-start | bytes 3145732
  102.3 13.6 %all-to-all-start.4 = ((bf16[4,64,1024]{2,1,0:T(8,128)(2,1)}), bf16[4,64,1024]{2,1,0:T(8,128)(2,1)S(1)}, u32[]{:S(2)}, u32[]{:S(2)}) async-start(bf16[4,64,1024]{2,1,0:T(8,128)(2,1)} %bitcast.17), calls=%async_computation.4 | async-start | bytes 1048576 | tf_op jit(solution)/shard_map/all_to_all | solution.py:25
  116.7 18.5 %all-to-all-start.5 = ((bf16[16,4,1024]{2,1,0:T(4,128)(2,1)}), bf16[16,4,1024]{2,1,0:T(4,128)(2,1)S(1)}, u32[]{:S(2)}, u32[]{:S(2)}) async-start(bf16[16,4,1024]{2,1,0:T(4,128)(2,1)} %reshape.23), calls=%async_computation.5 | async-start | bytes 262144 | tf_op jit(solution)/shard_map/all_to_all | solution.py:25
Sparse Core Ops, SparseCore 0:
  32.8 33.2 all-gather.1

commit v5 on v4

--- a/solution.py
+++ b/solution.py
@@ -9,6 +9,7 @@
 from jax.sharding import PartitionSpec as P
 
 Y = 4
+CORES = 2
 PANEL, SUB, LANES = 64, 8, 128
 VMEM_BYTES = 58 * 2**20
 
@@ -107,15 +108,23 @@
 
 
 def project_kernel(
-    gram_ref, sketch_hbm, activations_hbm, inverse_ref, out_ref,
-    work, sketch_ref, activations_ref, done, *, scale, depth, lines,
+    gram_ref, near_hbm, far_hbm, activations_hbm, basis_ref, out_ref,
+    work, inverse_ref, sketch_ref, activations_ref, done, *, scale, depth, lines,
 ):
-    fetches = [
-        pltpu.make_async_copy(sketch_hbm, sketch_ref, done.at[0]),
-        pltpu.make_async_copy(activations_hbm, activations_ref, done.at[1]),
-    ]
+    col = lax.axis_index("col")
+    chips, tokens = near_hbm.shape[:2]
+    chip, core = col // CORES, col % CORES
+    fetches = []
+    for step in range(chips):
+        for other, slices in enumerate((near_hbm, far_hbm)):
+            place = (chip + step) % chips * CORES + (core + other) % CORES
+            rows = pl.ds(pl.multiple_of(place * tokens, tokens), tokens)
+            at = done.at[CORES * step + other]
+            fetches.append(pltpu.make_async_copy(slices.at[step], sketch_ref.at[rows], at))
+    last = pltpu.make_async_copy(activations_hbm, activations_ref, done.at[CORES * chips])
     for fetch in fetches:
         fetch.start()
+    last.start()
     invert_factor(gram_ref, inverse_ref, work, scale)
     rank = gram_ref.shape[0]
     f32, bf16 = jnp.float32, jnp.bfloat16
@@ -123,44 +132,63 @@
     source = lax.broadcasted_iota(jnp.int32, (rank, rank), 1)
     y, z, line = to // (depth * lines), to // lines % depth, to % lines
     turn = (source == (z * Y + y) * lines + line).astype(bf16)
-    by_rows = (((1,), (1,)), ((), ()))
     turned = [
         jnp.dot(turn, part, preferred_element_type=f32).astype(bf16)
         for part in split(inverse_ref[...])
     ]
-    fetches[0].wait()
-    basis = sum(
-        lax.dot_general(part, sketch_ref[...], by_rows, preferred_element_type=f32)
-        for part in turned
-    ).astype(bf16)
-    fetches[1].wait()
+    for fetch in fetches:
+        fetch.wait()
+
+    def basis_of(parts):
+        by_rows = (((1,), (1,)), ((), ()))
+        terms = [
+            lax.dot_general(part, sketch_ref[...], by_rows, preferred_element_type=f32)
+            for part in parts
+        ]
+        return (terms[0] + terms[1]).astype(bf16)
+
+    width = basis_ref.shape[0]
+    mine = inverse_ref[pl.ds(pl.multiple_of(col * width, width), width), :]
+    basis_ref[...] = basis_of(split(mine))
+    basis = basis_of(turned)
+    last.wait()
     out_ref[...] = jnp.dot(basis, activations_ref[...], preferred_element_type=f32).astype(bf16)
 
 
-def project(gram, sketch, activations, scale, depth, lines):
+def project(gram, near, far, activations, scale, depth, lines):
     in_vmem, in_hbm = pl.BlockSpec(memory_space=pltpu.VMEM), pl.BlockSpec(memory_space=pltpu.HBM)
-    out = jax.ShapeDtypeStruct((gram.shape[0], activations.shape[1]), jnp.bfloat16)
+    rank, cols = gram.shape[0], lax.axis_size("col")
+    tokens, features = activations.shape
     return pl.pallas_call(
         functools.partial(project_kernel, scale=scale, depth=depth, lines=lines),
-        out_shape=[gram, out],
-        in_specs=[in_vmem, in_hbm, in_hbm],
+        out_shape=[
+            jax.ShapeDtypeStruct((rank // cols, tokens), jnp.bfloat16),
+            jax.ShapeDtypeStruct((rank, features), jnp.bfloat16),
+        ],
+        in_specs=[in_vmem, in_hbm, in_hbm, in_hbm],
         out_specs=[in_vmem, in_vmem],
         scratch_shapes=[
             pltpu.VMEM(gram.shape, jnp.float32),
-            pltpu.VMEM(sketch.shape, jnp.bfloat16),
+            pltpu.VMEM(gram.shape, jnp.float32),
+            pltpu.VMEM((tokens, rank), jnp.bfloat16),
             pltpu.VMEM(activations.shape, jnp.bfloat16),
-            pltpu.SemaphoreType.DMA((2,)),
+            pltpu.SemaphoreType.DMA((cols + 1,)),
         ],
         compiler_params=pltpu.CompilerParams(vmem_limit_bytes=VMEM_BYTES),
         name="project",
-    )(gram, sketch, activations)
-
-
-def apply_pair(sketch, high, low):
-    by_rows = (((1,), (1,)), ((), ()))
-    out = lax.dot_general(sketch, high, by_rows, preferred_element_type=jnp.float32)
-    out = out + lax.dot_general(sketch, low, by_rows, preferred_element_type=jnp.float32)
-    return out.astype(jnp.bfloat16)
+    )(gram, near, far, activations)
+
+
+def gather_sketch(own):
+    cols = lax.axis_size("col")
+    chips = cols // CORES
+    near = [own]
+    for step in range(1, chips):
+        pairs = [(c, (c - CORES * step) % cols) for c in range(cols)]
+        near.append(lax.ppermute(own, "col", pairs))
+    near = jnp.stack(near)
+    far = lax.ppermute(near, "col", [(c, c ^ 1) for c in range(cols)])
+    return near, far
 
 
 def local(activations, start_basis):
@@ -174,8 +202,7 @@
     partial = partial.astype(jnp.bfloat16).reshape(cols, rows_dev // cols, rank)
     parts = exchange(partial, "col")
     own = jnp.sum(parts.astype(jnp.float32), 0).astype(jnp.bfloat16)
-    sent = jnp.sum(lax.optimization_barrier(parts).astype(jnp.float32), 0).astype(jnp.bfloat16)
-    sketch = lax.all_gather(sent, "col", axis=0, tiled=True)
+    near, far = gather_sketch(own)
 
     gram = lax.dot_general(own, own, (((0,), (0,)), ((), ())), preferred_element_type=jnp.float32)
     gram = gram.reshape(plane_size, rank // plane_size, rank)
@@ -184,17 +211,14 @@
     gram = share(gram, plane_size, ("row", "col"), plane).reshape(rank, rank)
 
     lines = rank // rows
-    inverse, projected = project(gram, sketch, activations, root_tokens, depth, lines)
+    basis, projected = project(gram, near, far, activations, root_tokens, depth, lines)
     projected = projected.reshape(Y, rank // Y, -1)
     projected = jnp.sum(exchange(projected, "row", along_y).astype(jnp.float32), 0)
     projected = projected.astype(jnp.bfloat16).reshape(depth, lines, -1)
     projected = exchange(projected, "row", along_z).astype(jnp.float32)
     projected = jnp.sum(projected, 0) / root_tokens
 
-    width = rank // cols
-    first = lax.axis_index("col") * width
-    mine = split(lax.dynamic_slice_in_dim(inverse, first, width, 0))
-    return (apply_pair(sketch, *mine), projected)
+    return (basis.T, projected)
 
 
 def solution(mesh):

time: 143 us -> 135 us (0.944)
  starting transfers between devices: 8.36 us -> 38.9 us
  blocking collectives: 76.1 us -> 51.7 us
  between operations: 14.1 us -> 0.79 us
  matrix products: 6.64 us -> 4.32 us
  local copies, waits for them, and re-layouts: 1.83 us -> 3.29 us
    all_to_all x4 -> x3, blocking collectives: 76.1 us -> 51.7 us  [exchange(): return lax.all_to_all(blocks, axis, 0, 0, axis_index_groups=members)]
    all_to_all x2 -> x3, starting transfers between devices: 8.32 us -> 25.3 us  [exchange(): return lax.all_to_all(blocks, axis, 0, 0, axis_index_groups=members)]
    ppermute x0 -> x4, starting transfers between devices: none -> 13.6 us  [the longest x3 11.7 us: gather_sketch(): near.append(lax.ppermute(own, 'col', pairs))]
    dot_general x2 -> x0, matrix products: 3.01 us -> none  [the longest x1 1.85 us: apply_pair(): lax.dot_general(sketch, low, by_rows, preferred_element_type=jnp.float32)]
    all_to_all x2 -> x3, waiting for transfers between devices: 20.8 us -> 20.4 us  [exchange(): return lax.all_to_all(blocks, axis, 0, 0, axis_index_groups=members)]
  transfers between devices with their start and end apart: 3 -> 7, of which waited for: 2 -> 2; matrix products, arithmetic and copies ran while one was open for 2% -> 1% of each run, Pallas kernels for 0% -> 0%
where the time goes in v5:
time: 135 us; the launch traced here: 134 us
  blocking collectives  51.7 us (38%)
  starting transfers between devices  38.9 us (29%)
  waiting for transfers between devices  20.4 us (15%)
  Pallas kernels  13.7 us (10%)
  matrix products  4.32 us (3%)
  local copies, waits for them, and re-layouts  3.29 us (2%)
    all_to_all x3, blocking collectives, exchange(): return lax.all_to_all(blocks, axis, 0, 0, axis_index_groups=members)  51.7 us
    all_to_all x3, starting transfers between devices, exchange(): return lax.all_to_all(blocks, axis, 0, 0, axis_index_groups=members)  25.3 us
    all_to_all x3, waiting for transfers between devices, exchange(): return lax.all_to_all(blocks, axis, 0, 0, axis_index_groups=members)  20.4 us
    pallas_call x1, Pallas kernels, project(): pl.pallas_call(functools.partial(project_kernel, scale=scale, depth=depth...  13.7 us
    ppermute x3, starting transfers between devices, gather_sketch(): near.append(lax.ppermute(own, 'col', pairs))  11.7 us
    dot_general x1, matrix products, local(): jnp.dot(activations, start_basis, preferred_element_type=jnp.float32)  3.44 us
  transfers between devices with their start and end apart: 7, of which 2 were waited for; matrix products, arithmetic and copies ran while one was open for 1% of the time, Pallas kernels for 0%

profile of v5, /device:TPU:32, one launch (start us, length us, event | category | flops | bytes accessed | tf_op | source)
XLA Modules:
  0.0 134.2 jit_solution(9553569858454340872)
XLA Ops:
  0.6 0.0 copy-start
  0.6 1.0 copy-done
  1.7 3.4 %convolution_convert_fusion = bf16[2048,256]{1,0:T(8,128)(2,1)S(1)} fusion(bf16[2048,1024]{1,0:T(8,128)(2,1)} %activations_hbm.1, bf16[1024,256]{1,0:T(8,128)(2,1)S(1)} %copy-done), kind=kOutput, calls=%fused_computation | convolution fusion | flops 1074266112 | bytes 5767168 | tf_op jit(solution)/shard_map/dot_general | solution.py:201
  5.1 20.2 %all_to_all.30 = bf16[8,256,256]{2,1,0:T(8,128)(2,1)S(1)} all-to-all(bf16[8,256,256]{2,1,0:T(8,128)(2,1)S(1)} %bitcast.19), channel_id=1, replica_groups=mesh['row'=64,'col'=8] {'col'}, dimensions={0} | all-to-all | bytes 2097152 | tf_op jit(solution)/shard_map/all_to_all | solution.py:26
  25.3 0.1 reduce_sum.51
  25.5 0.1 copy.11
  25.6 0.9 fusion
  26.5 5.5 %all-to-all-start.1 = ((f32[32,8,256]{2,1,0:T(8,128)}), f32[32,8,256]{2,1,0:T(8,128)S(1)}, u32[]{:S(2)}, u32[]{:S(2)}) async-start(f32[32,8,256]{2,1,0:T(8,128)} %fusion), calls=%async_computation.1 | async-start | bytes 524288 | tf_op jit(solution)/shard_map/all_to_all | solution.py:26
  31.9 3.7 %collective-permute-start.2 = (bf16[256,256]{1,0:T(8,128)(2,1)S(1)}, bf16[256,256]{1,0:T(8,128)(2,1)S(1)}, u32[]{:S(2)}, u32[]{:S(2)}) collective-permute-start(bf16[256,256]{1,0:T(8,128)(2,1)S(1)} %reduce_sum.51), channel_id=1, source_target_pairs={{0,2},{1,3},{2,4},{3,5},{4,6},{5,7},{6,0},{7,1},{8,10},{9,11},{10,... | collective-permute-start | bytes 393224 | tf_op jit(solution)/shard_map/ppermute | solution.py:188
  35.6 4.6 %collective-permute-start.1 = (bf16[256,256]{1,0:T(8,128)(2,1)S(1)}, bf16[256,256]{1,0:T(8,128)(2,1)S(1)}, u32[]{:S(2)}, u32[]{:S(2)}) collective-permute-start(bf16[256,256]{1,0:T(8,128)(2,1)S(1)} %reduce_sum.51), channel_id=1, source_target_pairs={{0,4},{1,5},{2,6},{3,7},{4,0},{5,1},{6,2},{7,3},{8,12},{9,13},{10,... | collective-permute-start | bytes 393224 | tf_op jit(solution)/shard_map/ppermute | solution.py:188
  40.2 3.4 %collective-permute-start = (bf16[256,256]{1,0:T(8,128)(2,1)S(1)}, bf16[256,256]{1,0:T(8,128)(2,1)S(1)}, u32[]{:S(2)}, u32[]{:S(2)}) collective-permute-start(bf16[256,256]{1,0:T(8,128)(2,1)S(1)} %reduce_sum.51), channel_id=1, source_target_pairs={{0,6},{1,7},{2,0},{3,1},{4,2},{5,3},{6,4},{7,5},{8,14},{9,15},{10,... | collective-permute-start | bytes 393224 | tf_op jit(solution)/shard_map/ppermute | solution.py:188
  43.6 0.0 all-to-all-done.1
  43.7 0.7 broadcast_in_dim.4
  44.3 15.2 %all-to-all-start.2 = ((f32[16,8,256]{2,1,0:T(8,128)}), f32[16,8,256]{2,1,0:T(8,128)S(1)}, u32[]{:S(2)}, u32[]{:S(2)}) async-start(f32[16,8,256]{2,1,0:T(8,128)} %broadcast_in_dim.4), calls=%async_computation.2 | async-start | bytes 262144 | tf_op jit(solution)/shard_map/all_to_all | solution.py:26
  59.5 0.0 collective-permute-done.2
  59.5 0.0 collective-permute-done.1
  59.6 0.0 collective-permute-done
  59.6 0.1 pad_maximum_fusion.near_hbm
  59.6 0.0 copy-start.1
  59.7 1.9 %collective-permute-start.3 = (bf16[4,256,256]{2,1,0:T(8,128)(2,1)S(1)}, bf16[4,256,256]{2,1,0:T(8,128)(2,1)S(1)}, u32[]{:S(2)}, u32[]{:S(2)}) collective-permute-start(bf16[4,256,256]{2,1,0:T(8,128)(2,1)S(1)} %pad_maximum_fusion.near_hbm), channel_id=1, source_target_pairs={{0,1},{1,0},{2,3},{3,2},{4,5},{5,4},{6,7},{7,6},{8,9},{9,8},{10,11... | collective-permute-start | bytes 1572872 | tf_op jit(solution)/shard_map/ppermute | solution.py:190
  61.6 11.5 %all-to-all-done.2 = f32[16,8,256]{2,1,0:T(8,128)S(1)} async-done(((f32[16,8,256]{2,1,0:T(8,128)}), f32[16,8,256]{2,1,0:T(8,128)S(1)}, u32[]{:S(2)}, u32[]{:S(2)}) %all-to-all-start.2) | async-done | bytes 131104 | tf_op jit(solution)/shard_map/all_to_all | solution.py:26
  73.1 0.7 broadcast_in_dim.5
  73.8 4.7 %all-to-all-start.3 = ((f32[32,8,256]{2,1,0:T(8,128)}), f32[32,8,256]{2,1,0:T(8,128)S(1)}, u32[]{:S(2)}, u32[]{:S(2)}) async-start(f32[32,8,256]{2,1,0:T(8,128)} %broadcast_in_dim.5), calls=%async_computation.3 | async-start | bytes 524288 | tf_op jit(solution)/shard_map/all_to_all | solution.py:26
  78.5 0.0 collective-permute-done.3.far_hbm
  78.5 0.0 copy-start.3
  78.5 8.9 %all-to-all-done.3 = f32[32,8,256]{2,1,0:T(8,128)S(1)} async-done(((f32[32,8,256]{2,1,0:T(8,128)}), f32[32,8,256]{2,1,0:T(8,128)S(1)}, u32[]{:S(2)}, u32[]{:S(2)}) %all-to-all-start.3) | async-done | bytes 262176 | tf_op jit(solution)/shard_map/all_to_all | solution.py:26
  87.4 0.0 copy-start.2
  87.4 0.0 copy-done.1
  87.4 0.0 copy-done.3
  87.4 0.7 copy-done.2
  88.1 13.7 %project.1 = (bf16[32,2048]{1,0:T(8,128)(2,1)}, bf16[256,1024]{1,0:T(8,128)(2,1)}) custom-call(f32[256,256]{1,0:T(8,128)} %bitcast.20, bf16[4,256,256]{2,1,0:T(8,128)(2,1)} %copy-done.1, bf16[4,256,256]{2,1,0:T(8,128)(2,1)} %copy-done.3, bf16[2048,1024]{1,0:T(8,128)(2,1)} %activations_hbm.1), custom_call_target="tpu_custom_call" | custom-call | tf_op jit(solution)/shard_map/project/pallas_call | solution.py:162
  101.8 13.6 %all_to_all.31 = bf16[4,64,1024]{2,1,0:T(8,128)(2,1)S(1)} all-to-all(bf16[4,64,1024]{2,1,0:T(8,128)(2,1)} %bitcast.21), channel_id=1, replica_groups={{0,8,16,24},{32,40,48,56},{64,72,80,88},{96,104,112,120},{128,136,144,1..., dimensions={0} | all-to-all | bytes 1048576 | tf_op jit(solution)/shard_map/all_to_all | solution.py:26
  115.5 0.1 reduce_sum.54
  115.6 0.1 reshape.23
  115.6 17.9 %all_to_all.32 = bf16[16,4,1024]{2,1,0:T(4,128)(2,1)S(1)} all-to-all(bf16[16,4,1024]{2,1,0:T(4,128)(2,1)S(1)} %reshape.23), channel_id=1, replica_groups={{0,32,64,96,128,160,192,224,256,288,320,352,384,416,448,480},{8,40,72,1..., dimensions={0} | all-to-all | bytes 262144 | tf_op jit(solution)/shard_map/all_to_all | solution.py:26
  133.5 0.1 convert_reduce_fusion
  133.6 0.6 broadcast_multiply_fusion
  (2 shorter events, 0.1 us)
Async XLA Ops:
  0.6 1.0 copy-start
  26.5 17.1 %all-to-all-start.1 = ((f32[32,8,256]{2,1,0:T(8,128)}), f32[32,8,256]{2,1,0:T(8,128)S(1)}, u32[]{:S(2)}, u32[]{:S(2)}) async-start(f32[32,8,256]{2,1,0:T(8,128)} %fusion), calls=%async_computation.1 | async-start | bytes 524288 | tf_op jit(solution)/shard_map/all_to_all | solution.py:26
  31.9 27.6 %collective-permute-start.2 = (bf16[256,256]{1,0:T(8,128)(2,1)S(1)}, bf16[256,256]{1,0:T(8,128)(2,1)S(1)}, u32[]{:S(2)}, u32[]{:S(2)}) collective-permute-start(bf16[256,256]{1,0:T(8,128)(2,1)S(1)} %reduce_sum.51), channel_id=1, source_target_pairs={{0,2},{1,3},{2,4},{3,5},{4,6},{5,7},{6,0},{7,1},{8,10},{9,11},{10,... | collective-permute-start | bytes 393224 | tf_op jit(solution)/shard_map/ppermute | solution.py:188
  35.6 23.9 %collective-permute-start.1 = (bf16[256,256]{1,0:T(8,128)(2,1)S(1)}, bf16[256,256]{1,0:T(8,128)(2,1)S(1)}, u32[]{:S(2)}, u32[]{:S(2)}) collective-permute-start(bf16[256,256]{1,0:T(8,128)(2,1)S(1)} %reduce_sum.51), channel_id=1, source_target_pairs={{0,4},{1,5},{2,6},{3,7},{4,0},{5,1},{6,2},{7,3},{8,12},{9,13},{10,... | collective-permute-start | bytes 393224 | tf_op jit(solution)/shard_map/ppermute | solution.py:188
  40.2 19.3 %collective-permute-start = (bf16[256,256]{1,0:T(8,128)(2,1)S(1)}, bf16[256,256]{1,0:T(8,128)(2,1)S(1)}, u32[]{:S(2)}, u32[]{:S(2)}) collective-permute-start(bf16[256,256]{1,0:T(8,128)(2,1)S(1)} %reduce_sum.51), channel_id=1, source_target_pairs={{0,6},{1,7},{2,0},{3,1},{4,2},{5,3},{6,4},{7,5},{8,14},{9,15},{10,... | collective-permute-start | bytes 393224 | tf_op jit(solution)/shard_map/ppermute | solution.py:188
  44.3 28.7 %all-to-all-start.2 = ((f32[16,8,256]{2,1,0:T(8,128)}), f32[16,8,256]{2,1,0:T(8,128)S(1)}, u32[]{:S(2)}, u32[]{:S(2)}) async-start(f32[16,8,256]{2,1,0:T(8,128)} %broadcast_in_dim.4), calls=%async_computation.2 | async-start | bytes 262144 | tf_op jit(solution)/shard_map/all_to_all | solution.py:26
  59.6 27.7 %copy-start.1 = (bf16[4,256,256]{2,1,0:T(8,128)(2,1)}, bf16[4,256,256]{2,1,0:T(8,128)(2,1)S(1)}, u32[]{:S(2)}) copy-start(bf16[4,256,256]{2,1,0:T(8,128)(2,1)S(1)} %pad_maximum_fusion.near_hbm) | copy-start | bytes 1572868
  59.7 18.8 %collective-permute-start.3 = (bf16[4,256,256]{2,1,0:T(8,128)(2,1)S(1)}, bf16[4,256,256]{2,1,0:T(8,128)(2,1)S(1)}, u32[]{:S(2)}, u32[]{:S(2)}) collective-permute-start(bf16[4,256,256]{2,1,0:T(8,128)(2,1)S(1)} %pad_maximum_fusion.near_hbm), channel_id=1, source_target_pairs={{0,1},{1,0},{2,3},{3,2},{4,5},{5,4},{6,7},{7,6},{8,9},{9,8},{10,11... | collective-permute-start | bytes 1572872 | tf_op jit(solution)/shard_map/ppermute | solution.py:190
  73.8 13.6 %all-to-all-start.3 = ((f32[32,8,256]{2,1,0:T(8,128)}), f32[32,8,256]{2,1,0:T(8,128)S(1)}, u32[]{:S(2)}, u32[]{:S(2)}) async-start(f32[32,8,256]{2,1,0:T(8,128)} %broadcast_in_dim.5), calls=%async_computation.3 | async-start | bytes 524288 | tf_op jit(solution)/shard_map/all_to_all | solution.py:26
  78.5 8.9 %copy-start.3 = (bf16[4,256,256]{2,1,0:T(8,128)(2,1)}, bf16[4,256,256]{2,1,0:T(8,128)(2,1)S(1)}, u32[]{:S(2)}) copy-start(bf16[4,256,256]{2,1,0:T(8,128)(2,1)S(1)} %collective-permute-done.3.far_hbm) | copy-start | bytes 1572868
  87.4 0.7 copy-start.2

commit v6 on v5

--- a/solution.py
+++ b/solution.py
@@ -19,7 +19,8 @@
     plane = [[(z * Y + y) * cols + c for y in range(Y) for c in range(cols)] for z in range(depth)]
     along_z = [[z * Y + y for z in range(depth)] for y in range(Y)]
     along_y = [[z * Y + y for y in range(Y)] for z in range(depth)]
-    return plane, along_y, along_z
+    along_x = [list(range(core, cols, CORES)) for core in range(CORES)]
+    return plane, along_x, along_y, along_z
 
 
 def exchange(blocks, axis, members=None):
@@ -117,7 +118,7 @@
     fetches = []
     for step in range(chips):
         for other, slices in enumerate((near_hbm, far_hbm)):
-            place = (chip + step) % chips * CORES + (core + other) % CORES
+            place = (core + other) % CORES * chips + (chip + step) % chips
             rows = pl.ds(pl.multiple_of(place * tokens, tokens), tokens)
             at = done.at[CORES * step + other]
             fetches.append(pltpu.make_async_copy(slices.at[step], sketch_ref.at[rows], at))
@@ -179,34 +180,39 @@
     )(gram, near, far, activations)
 
 
-def gather_sketch(own):
+def from_chip(own, step):
     cols = lax.axis_size("col")
-    chips = cols // CORES
-    near = [own]
-    for step in range(1, chips):
-        pairs = [(c, (c - CORES * step) % cols) for c in range(cols)]
-        near.append(lax.ppermute(own, "col", pairs))
-    near = jnp.stack(near)
-    far = lax.ppermute(near, "col", [(c, c ^ 1) for c in range(cols)])
-    return near, far
+    return lax.ppermute(own, "col", [(c, (c - CORES * step) % cols) for c in range(cols)])
 
 
 def local(activations, start_basis):
     rows, cols = lax.axis_size("row"), lax.axis_size("col")
     rows_dev, rank = activations.shape[0], start_basis.shape[1]
     root_tokens = math.sqrt(rows_dev * rows)
-    plane, along_y, along_z = groups(rows, cols)
+    plane, along_x, along_y, along_z = groups(rows, cols)
     plane_size, depth = Y * cols, rows // Y
 
-    partial = jnp.dot(activations, start_basis, preferred_element_type=jnp.float32)
-    partial = partial.astype(jnp.bfloat16).reshape(cols, rows_dev // cols, rank)
-    parts = exchange(partial, "col")
+    half, core = rows_dev // CORES, lax.axis_index("col") % CORES
+
+    def half_sketch(index):
+        block = lax.dynamic_slice_in_dim(activations, index * half, half, 0)
+        return jnp.dot(block, start_basis, preferred_element_type=jnp.float32)
+
+    other = half_sketch(1 - core).astype(jnp.bfloat16)
+    other = lax.ppermute(other, "col", [(c, c ^ 1) for c in range(cols)])
+    mine = lax.optimization_barrier(half_sketch(core))
+    partial = (mine + other.astype(jnp.float32)).astype(jnp.bfloat16)
+    partial = partial.reshape(cols // CORES, -1, rank)
+    parts = exchange(partial, "col", along_x)
     own = jnp.sum(parts.astype(jnp.float32), 0).astype(jnp.bfloat16)
-    near, far = gather_sketch(own)
+    first_near = [own] + [from_chip(own, step) for step in range(1, cols // CORES - 1)]
 
     gram = lax.dot_general(own, own, (((0,), (0,)), ((), ())), preferred_element_type=jnp.float32)
     gram = gram.reshape(plane_size, rank // plane_size, rank)
     gram = jnp.sum(exchange(gram, ("row", "col"), plane), 0)
+    late, _ = lax.optimization_barrier((own, gram))
+    near = jnp.stack(first_near + [from_chip(late, cols // CORES - 1)])
+    far = lax.ppermute(near, "col", [(c, c ^ 1) for c in range(cols)])
     gram = jnp.sum(share(gram, depth, "row", along_z), 0)
     gram = share(gram, plane_size, ("row", "col"), plane).reshape(rank, rank)
 

time: 135 us -> 133 us (0.985)
  blocking collectives: 51.7 us -> 45.8 us
  starting transfers between devices: 38.9 us -> 41.2 us
    all_to_all x3, blocking collectives: 51.7 us -> 45.8 us  [exchange(): return lax.all_to_all(blocks, axis, 0, 0, axis_index_groups=members)]
    dot_general x1 -> x2, matrix products: 3.44 us -> 4.6 us  [half_sketch(): return jnp.dot(block, start_basis, preferred_element_type=jnp.float32)]
    ppermute x4 -> x5, starting transfers between devices: 13.6 us -> 14.6 us  [the longest x3 10.8 us: from_chip(): lax.ppermute(own, 'col', [(c, (c - CORES * step) % cols) for c in range(c...]
  transfers between devices with their start and end apart: 7 -> 8, of which waited for: 2 -> 3; matrix products, arithmetic and copies ran while one was open for 1% -> 3% of each run, Pallas kernels for 0% -> 0%
where the time goes in v6:
time: 133 us
  blocking collectives  45.8 us (34%)
  starting transfers between devices  41.2 us (31%)
  waiting for transfers between devices  21.3 us (16%)
  Pallas kernels  13.7 us (10%)
  matrix products  5.48 us (4%)
  local copies, waits for them, and re-layouts  3.29 us (2%)
    all_to_all x3, blocking collectives, exchange(): return lax.all_to_all(blocks, axis, 0, 0, axis_index_groups=members)  45.8 us
    all_to_all x3, starting transfers between devices, exchange(): return lax.all_to_all(blocks, axis, 0, 0, axis_index_groups=members)  26.6 us
    all_to_all x3, waiting for transfers between devices, exchange(): return lax.all_to_all(blocks, axis, 0, 0, axis_index_groups=members)  21.3 us
    pallas_call x1, Pallas kernels, project(): pl.pallas_call(functools.partial(project_kernel, scale=scale, depth=depth...  13.7 us
    ppermute x3, starting transfers between devices, from_chip(): lax.ppermute(own, 'col', [(c, (c - CORES * step) % cols) for c in range(c...  10.8 us
    dot_general x2, matrix products, half_sketch(): return jnp.dot(block, start_basis, preferred_element_type=jnp.float32)  4.6 us
  transfers between devices with their start and end apart: 8, of which 3 were waited for; matrix products, arithmetic and copies ran while one was open for 3% of the time, Pallas kernels for 0%

profile of v6, /device:TPU:32, one launch (start us, length us, event | category | flops | bytes accessed | tf_op | source)
XLA Modules:
  0.0 132.7 jit_solution(2348529739238705243)
XLA Ops:
  0.6 0.0 copy-start
  0.7 1.0 copy-done
  1.7 2.3 %fusion.4 = bf16[1024,256]{1,0:T(8,128)(2,1)S(1)} fusion(bf16[1024,256]{1,0:T(8,128)(2,1)S(1)} %copy-done, bf16[2048,1024]{1,0:T(8,128)(2,1)} %activations_hbm.1, s32[]{:T(128)S(6)} %select_n.15), kind=kOutput, calls=%fused_computation.4 | convolution fusion | flops 537133056 | bytes 3145732 | tf_op jit(solution)/shard_map/dot_general | solution.py:199
  4.0 1.9 %collective-permute-start = (bf16[1024,256]{1,0:T(8,128)(2,1)S(1)}, bf16[1024,256]{1,0:T(8,128)(2,1)S(1)}, u32[]{:S(2)}, u32[]{:S(2)}) collective-permute-start(bf16[1024,256]{1,0:T(8,128)(2,1)S(1)} %fusion.4), channel_id=1, source_target_pairs={{0,1},{1,0},{2,3},{3,2},{4,5},{5,4},{6,7},{7,6},{8,9},{9,8},{10,11... | collective-permute-start | bytes 1572872 | tf_op jit(solution)/shard_map/ppermute | solution.py:202
  5.9 2.3 %fusion.2 = f32[1024,256]{1,0:T(8,128)S(1)} fusion(bf16[1024,256]{1,0:T(8,128)(2,1)S(1)} %copy-done, bf16[2048,1024]{1,0:T(8,128)(2,1)} %activations_hbm.1, s32[]{:T(128)S(6)} %select_n.14), kind=kOutput, calls=%fused_computation.2 | convolution fusion | flops 536870912 | bytes 3670020 | tf_op jit(solution)/shard_map/dot_general | solution.py:199
  8.2 0.0 collective-permute-done
  8.2 0.1 add_convert_fusion
  8.4 14.2 %all_to_all.30 = bf16[4,256,256]{2,1,0:T(8,128)(2,1)S(1)} all-to-all(bf16[4,256,256]{2,1,0:T(8,128)(2,1)S(1)} %bitcast.17), channel_id=1, replica_groups={{0,2,4,6},{1,3,5,7},{8,10,12,14},{9,11,13,15},{16,18,20,22},{17,19,21,2..., dimensions={0} | all-to-all | bytes 1048576 | tf_op jit(solution)/shard_map/all_to_all | solution.py:27
  22.6 0.1 reduce_sum.51
  22.7 0.1 copy.11
  22.8 0.9 fusion.7
  23.7 5.5 %all-to-all-start.1 = ((f32[32,8,256]{2,1,0:T(8,128)}), f32[32,8,256]{2,1,0:T(8,128)S(1)}, u32[]{:S(2)}, u32[]{:S(2)}) async-start(f32[32,8,256]{2,1,0:T(8,128)} %fusion.7), calls=%async_computation.1 | async-start | bytes 524288 | tf_op jit(solution)/shard_map/all_to_all | solution.py:27
  29.1 5.2 %collective-permute-start.2 = (bf16[256,256]{1,0:T(8,128)(2,1)S(1)}, bf16[256,256]{1,0:T(8,128)(2,1)S(1)}, u32[]{:S(2)}, u32[]{:S(2)}) collective-permute-start(bf16[256,256]{1,0:T(8,128)(2,1)S(1)} %reduce_sum.51), channel_id=1, source_target_pairs={{0,4},{1,5},{2,6},{3,7},{4,0},{5,1},{6,2},{7,3},{8,12},{9,13},{10,... | collective-permute-start | bytes 393224 | tf_op jit(solution)/shard_map/ppermute | solution.py:185
  34.3 3.1 %collective-permute-start.1 = (bf16[256,256]{1,0:T(8,128)(2,1)S(1)}, bf16[256,256]{1,0:T(8,128)(2,1)S(1)}, u32[]{:S(2)}, u32[]{:S(2)}) collective-permute-start(bf16[256,256]{1,0:T(8,128)(2,1)S(1)} %reduce_sum.51), channel_id=1, source_target_pairs={{0,6},{1,7},{2,0},{3,1},{4,2},{5,3},{6,4},{7,5},{8,14},{9,15},{10,... | collective-permute-start | bytes 393224 | tf_op jit(solution)/shard_map/ppermute | solution.py:185
  37.4 0.6 all-to-all-done.1
  38.1 2.5 %collective-permute-start.3 = (bf16[256,256]{1,0:T(8,128)(2,1)S(1)}, bf16[256,256]{1,0:T(8,128)(2,1)S(1)}, u32[]{:S(2)}, u32[]{:S(2)}) collective-permute-start(bf16[256,256]{1,0:T(8,128)(2,1)S(1)} %reduce_sum.51), channel_id=1, source_target_pairs={{0,2},{1,3},{2,4},{3,5},{4,6},{5,7},{6,0},{7,1},{8,10},{9,11},{10,... | collective-permute-start | bytes 393224 | tf_op jit(solution)/shard_map/ppermute | solution.py:185
  40.6 0.7 broadcast_in_dim.4
  41.2 15.2 %all-to-all-start.2 = ((f32[16,8,256]{2,1,0:T(8,128)}), f32[16,8,256]{2,1,0:T(8,128)S(1)}, u32[]{:S(2)}, u32[]{:S(2)}) async-start(f32[16,8,256]{2,1,0:T(8,128)} %broadcast_in_dim.4), calls=%async_computation.2 | async-start | bytes 262144 | tf_op jit(solution)/shard_map/all_to_all | solution.py:27
  56.4 0.0 collective-permute-done.2
  56.5 0.0 collective-permute-done.1
  56.5 0.0 collective-permute-done.3
  56.5 0.1 pad_maximum_fusion.near_hbm
  56.6 0.0 copy-start.1
  56.6 1.9 %collective-permute-start.4 = (bf16[4,256,256]{2,1,0:T(8,128)(2,1)S(1)}, bf16[4,256,256]{2,1,0:T(8,128)(2,1)S(1)}, u32[]{:S(2)}, u32[]{:S(2)}) collective-permute-start(bf16[4,256,256]{2,1,0:T(8,128)(2,1)S(1)} %pad_maximum_fusion.near_hbm), channel_id=1, source_target_pairs={{0,1},{1,0},{2,3},{3,2},{4,5},{5,4},{6,7},{7,6},{8,9},{9,8},{10,11... | collective-permute-start | bytes 1572872 | tf_op jit(solution)/shard_map/ppermute | solution.py:215
  58.5 11.8 %all-to-all-done.2 = f32[16,8,256]{2,1,0:T(8,128)S(1)} async-done(((f32[16,8,256]{2,1,0:T(8,128)}), f32[16,8,256]{2,1,0:T(8,128)S(1)}, u32[]{:S(2)}, u32[]{:S(2)}) %all-to-all-start.2) | async-done | bytes 131104 | tf_op jit(solution)/shard_map/all_to_all | solution.py:27
  70.3 0.7 broadcast_in_dim.5
  71.1 5.9 %all-to-all-start.3 = ((f32[32,8,256]{2,1,0:T(8,128)}), f32[32,8,256]{2,1,0:T(8,128)S(1)}, u32[]{:S(2)}, u32[]{:S(2)}) async-start(f32[32,8,256]{2,1,0:T(8,128)} %broadcast_in_dim.5), calls=%async_computation.3 | async-start | bytes 524288 | tf_op jit(solution)/shard_map/all_to_all | solution.py:27
  77.0 0.0 collective-permute-done.4.far_hbm
  77.0 0.0 copy-start.3
  77.0 8.9 %all-to-all-done.3 = f32[32,8,256]{2,1,0:T(8,128)S(1)} async-done(((f32[32,8,256]{2,1,0:T(8,128)}), f32[32,8,256]{2,1,0:T(8,128)S(1)}, u32[]{:S(2)}, u32[]{:S(2)}) %all-to-all-start.3) | async-done | bytes 262176 | tf_op jit(solution)/shard_map/all_to_all | solution.py:27
  85.9 0.0 copy-start.2
  85.9 0.0 copy-done.1
  85.9 0.0 copy-done.3
  85.9 0.7 copy-done.2
  86.6 13.7 %project.1 = (bf16[32,2048]{1,0:T(8,128)(2,1)}, bf16[256,1024]{1,0:T(8,128)(2,1)}) custom-call(f32[256,256]{1,0:T(8,128)} %bitcast.20, bf16[4,256,256]{2,1,0:T(8,128)(2,1)} %copy-done.1, bf16[4,256,256]{2,1,0:T(8,128)(2,1)} %copy-done.3, bf16[2048,1024]{1,0:T(8,128)(2,1)} %activations_hbm.1), custom_call_target="tpu_custom_call" | custom-call | tf_op jit(solution)/shard_map/project/pallas_call | solution.py:163
  100.3 13.6 %all_to_all.31 = bf16[4,64,1024]{2,1,0:T(8,128)(2,1)S(1)} all-to-all(bf16[4,64,1024]{2,1,0:T(8,128)(2,1)} %bitcast.21), channel_id=1, replica_groups={{0,8,16,24},{32,40,48,56},{64,72,80,88},{96,104,112,120},{128,136,144,1..., dimensions={0} | all-to-all | bytes 1048576 | tf_op jit(solution)/shard_map/all_to_all | solution.py:27
  114.0 0.1 reduce_sum.54
  114.1 0.1 reshape.23
  114.1 17.9 %all_to_all.32 = bf16[16,4,1024]{2,1,0:T(4,128)(2,1)S(1)} all-to-all(bf16[16,4,1024]{2,1,0:T(4,128)(2,1)S(1)} %reshape.23), channel_id=1, replica_groups={{0,32,64,96,128,160,192,224,256,288,320,352,384,416,448,480},{8,40,72,1..., dimensions={0} | all-to-all | bytes 262144 | tf_op jit(solution)/shard_map/all_to_all | solution.py:27
  132.0 0.1 convert_reduce_fusion
  132.1 0.6 broadcast_multiply_fusion
  (2 shorter events, 0.1 us)
Async XLA Ops:
  0.6 1.0 copy-start
  4.0 4.3 %collective-permute-start = (bf16[1024,256]{1,0:T(8,128)(2,1)S(1)}, bf16[1024,256]{1,0:T(8,128)(2,1)S(1)}, u32[]{:S(2)}, u32[]{:S(2)}) collective-permute-start(bf16[1024,256]{1,0:T(8,128)(2,1)S(1)} %fusion.4), channel_id=1, source_target_pairs={{0,1},{1,0},{2,3},{3,2},{4,5},{5,4},{6,7},{7,6},{8,9},{9,8},{10,11... | collective-permute-start | bytes 1572872 | tf_op jit(solution)/shard_map/ppermute | solution.py:202
  23.7 14.4 %all-to-all-start.1 = ((f32[32,8,256]{2,1,0:T(8,128)}), f32[32,8,256]{2,1,0:T(8,128)S(1)}, u32[]{:S(2)}, u32[]{:S(2)}) async-start(f32[32,8,256]{2,1,0:T(8,128)} %fusion.7), calls=%async_computation.1 | async-start | bytes 524288 | tf_op jit(solution)/shard_map/all_to_all | solution.py:27
  29.1 27.3 %collective-permute-start.2 = (bf16[256,256]{1,0:T(8,128)(2,1)S(1)}, bf16[256,256]{1,0:T(8,128)(2,1)S(1)}, u32[]{:S(2)}, u32[]{:S(2)}) collective-permute-start(bf16[256,256]{1,0:T(8,128)(2,1)S(1)} %reduce_sum.51), channel_id=1, source_target_pairs={{0,4},{1,5},{2,6},{3,7},{4,0},{5,1},{6,2},{7,3},{8,12},{9,13},{10,... | collective-permute-start | bytes 393224 | tf_op jit(solution)/shard_map/ppermute | solution.py:185
  34.3 22.1 %collective-permute-start.1 = (bf16[256,256]{1,0:T(8,128)(2,1)S(1)}, bf16[256,256]{1,0:T(8,128)(2,1)S(1)}, u32[]{:S(2)}, u32[]{:S(2)}) collective-permute-start(bf16[256,256]{1,0:T(8,128)(2,1)S(1)} %reduce_sum.51), channel_id=1, source_target_pairs={{0,6},{1,7},{2,0},{3,1},{4,2},{5,3},{6,4},{7,5},{8,14},{9,15},{10,... | collective-permute-start | bytes 393224 | tf_op jit(solution)/shard_map/ppermute | solution.py:185
  38.1 18.4 %collective-permute-start.3 = (bf16[256,256]{1,0:T(8,128)(2,1)S(1)}, bf16[256,256]{1,0:T(8,128)(2,1)S(1)}, u32[]{:S(2)}, u32[]{:S(2)}) collective-permute-start(bf16[256,256]{1,0:T(8,128)(2,1)S(1)} %reduce_sum.51), channel_id=1, source_target_pairs={{0,2},{1,3},{2,4},{3,5},{4,6},{5,7},{6,0},{7,1},{8,10},{9,11},{10,... | collective-permute-start | bytes 393224 | tf_op jit(solution)/shard_map/ppermute | solution.py:185
  41.2 29.1 %all-to-all-start.2 = ((f32[16,8,256]{2,1,0:T(8,128)}), f32[16,8,256]{2,1,0:T(8,128)S(1)}, u32[]{:S(2)}, u32[]{:S(2)}) async-start(f32[16,8,256]{2,1,0:T(8,128)} %broadcast_in_dim.4), calls=%async_computation.2 | async-start | bytes 262144 | tf_op jit(solution)/shard_map/all_to_all | solution.py:27
  56.6 29.3 %copy-start.1 = (bf16[4,256,256]{2,1,0:T(8,128)(2,1)}, bf16[4,256,256]{2,1,0:T(8,128)(2,1)S(1)}, u32[]{:S(2)}) copy-start(bf16[4,256,256]{2,1,0:T(8,128)(2,1)S(1)} %pad_maximum_fusion.near_hbm) | copy-start | bytes 1572868
  56.6 20.4 %collective-permute-start.4 = (bf16[4,256,256]{2,1,0:T(8,128)(2,1)S(1)}, bf16[4,256,256]{2,1,0:T(8,128)(2,1)S(1)}, u32[]{:S(2)}, u32[]{:S(2)}) collective-permute-start(bf16[4,256,256]{2,1,0:T(8,128)(2,1)S(1)} %pad_maximum_fusion.near_hbm), channel_id=1, source_target_pairs={{0,1},{1,0},{2,3},{3,2},{4,5},{5,4},{6,7},{7,6},{8,9},{9,8},{10,11... | collective-permute-start | bytes 1572872 | tf_op jit(solution)/shard_map/ppermute | solution.py:215
  71.1 14.8 %all-to-all-start.3 = ((f32[32,8,256]{2,1,0:T(8,128)}), f32[32,8,256]{2,1,0:T(8,128)S(1)}, u32[]{:S(2)}, u32[]{:S(2)}) async-start(f32[32,8,256]{2,1,0:T(8,128)} %broadcast_in_dim.5), calls=%async_computation.3 | async-start | bytes 524288 | tf_op jit(solution)/shard_map/all_to_all | solution.py:27
  77.0 8.9 %copy-start.3 = (bf16[4,256,256]{2,1,0:T(8,128)(2,1)}, bf16[4,256,256]{2,1,0:T(8,128)(2,1)S(1)}, u32[]{:S(2)}) copy-start(bf16[4,256,256]{2,1,0:T(8,128)(2,1)S(1)} %collective-permute-done.4.far_hbm) | copy-start | bytes 1572868
  85.9 0.7 copy-start.2

commit v7 on v6

--- a/solution.py
+++ b/solution.py
@@ -11,7 +11,7 @@
 Y = 4
 CORES = 2
 PANEL, SUB, LANES = 64, 8, 128
-VMEM_BYTES = 58 * 2**20
+VMEM_BYTES = 52 * 2**20
 
 
 def groups(rows, cols):
@@ -153,7 +153,8 @@
     basis_ref[...] = basis_of(split(mine))
     basis = basis_of(turned)
     last.wait()
-    out_ref[...] = jnp.dot(basis, activations_ref[...], preferred_element_type=f32).astype(bf16)
+    projected = jnp.dot(basis, activations_ref[...], preferred_element_type=f32)
+    out_ref[...] = (projected * (1.0 / scale)).astype(bf16)
 
 
 def project(gram, near, far, activations, scale, depth, lines):
@@ -222,7 +223,7 @@
     projected = jnp.sum(exchange(projected, "row", along_y).astype(jnp.float32), 0)
     projected = projected.astype(jnp.bfloat16).reshape(depth, lines, -1)
     projected = exchange(projected, "row", along_z).astype(jnp.float32)
-    projected = jnp.sum(projected, 0) / root_tokens
+    projected = jnp.sum(projected, 0)
 
     return (basis.T, projected)
 

time: 133 us -> 131 us (0.985)
  no operation moved by 1% of the time
where the time goes in v7:
time: 131 us; the launch traced here: 130 us
  blocking collectives  44.7 us (34%)
  starting transfers between devices  41.2 us (31%)
  waiting for transfers between devices  21.4 us (16%)
  Pallas kernels  13.3 us (10%)
  matrix products  5.48 us (4%)
  local copies, waits for them, and re-layouts  2.56 us (2%)
    all_to_all x3, blocking collectives, exchange(): return lax.all_to_all(blocks, axis, 0, 0, axis_index_groups=members)  44.7 us
    all_to_all x3, starting transfers between devices, exchange(): return lax.all_to_all(blocks, axis, 0, 0, axis_index_groups=members)  26.6 us
    all_to_all x3, waiting for transfers between devices, exchange(): return lax.all_to_all(blocks, axis, 0, 0, axis_index_groups=members)  21.3 us
    pallas_call x1, Pallas kernels, project(): pl.pallas_call(functools.partial(project_kernel, scale=scale, depth=depth...  13.3 us
    ppermute x3, starting transfers between devices, from_chip(): lax.ppermute(own, 'col', [(c, (c - CORES * step) % cols) for c in range(c...  10.8 us
    dot_general x2, matrix products, half_sketch(): return jnp.dot(block, start_basis, preferred_element_type=jnp.float32)  4.6 us
  transfers between devices with their start and end apart: 8, of which 3 were waited for; matrix products, arithmetic and copies ran while one was open for 3% of the time, Pallas kernels for 0%

profile of v7, /device:TPU:32, one launch (start us, length us, event | category | flops | bytes accessed | tf_op | source)
XLA Modules:
  0.0 130.5 jit_solution(3049072293952970947)
XLA Ops:
  0.6 0.0 copy-start
  0.7 1.0 copy-done
  1.7 2.3 %fusion.4 = bf16[1024,256]{1,0:T(8,128)(2,1)S(1)} fusion(bf16[1024,256]{1,0:T(8,128)(2,1)S(1)} %copy-done, bf16[2048,1024]{1,0:T(8,128)(2,1)} %activations_hbm.1, s32[]{:T(128)S(6)} %select_n.15), kind=kOutput, calls=%fused_computation.4 | convolution fusion | flops 537133056 | bytes 3145732 | tf_op jit(solution)/shard_map/dot_general | solution.py:200
  4.0 1.9 %collective-permute-start = (bf16[1024,256]{1,0:T(8,128)(2,1)S(1)}, bf16[1024,256]{1,0:T(8,128)(2,1)S(1)}, u32[]{:S(2)}, u32[]{:S(2)}) collective-permute-start(bf16[1024,256]{1,0:T(8,128)(2,1)S(1)} %fusion.4), channel_id=1, source_target_pairs={{0,1},{1,0},{2,3},{3,2},{4,5},{5,4},{6,7},{7,6},{8,9},{9,8},{10,11... | collective-permute-start | bytes 1572872 | tf_op jit(solution)/shard_map/ppermute | solution.py:203
  5.9 2.3 %fusion.2 = f32[1024,256]{1,0:T(8,128)S(1)} fusion(bf16[1024,256]{1,0:T(8,128)(2,1)S(1)} %copy-done, bf16[2048,1024]{1,0:T(8,128)(2,1)} %activations_hbm.1, s32[]{:T(128)S(6)} %select_n.14), kind=kOutput, calls=%fused_computation.2 | convolution fusion | flops 536870912 | bytes 3670020 | tf_op jit(solution)/shard_map/dot_general | solution.py:200
  8.2 0.0 collective-permute-done
  8.2 0.1 add_convert_fusion
  8.4 14.2 %all_to_all.30 = bf16[4,256,256]{2,1,0:T(8,128)(2,1)S(1)} all-to-all(bf16[4,256,256]{2,1,0:T(8,128)(2,1)S(1)} %bitcast.19), channel_id=1, replica_groups={{0,2,4,6},{1,3,5,7},{8,10,12,14},{9,11,13,15},{16,18,20,22},{17,19,21,2..., dimensions={0} | all-to-all | bytes 1048576 | tf_op jit(solution)/shard_map/all_to_all | solution.py:27
  22.6 0.1 reduce_sum.51
  22.7 0.1 copy.11
  22.8 0.9 fusion.7
  23.7 5.5 %all-to-all-start.1 = ((f32[32,8,256]{2,1,0:T(8,128)}), f32[32,8,256]{2,1,0:T(8,128)S(1)}, u32[]{:S(2)}, u32[]{:S(2)}) async-start(f32[32,8,256]{2,1,0:T(8,128)} %fusion.7), calls=%async_computation.1 | async-start | bytes 524288 | tf_op jit(solution)/shard_map/all_to_all | solution.py:27
  29.1 5.2 %collective-permute-start.2 = (bf16[256,256]{1,0:T(8,128)(2,1)S(1)}, bf16[256,256]{1,0:T(8,128)(2,1)S(1)}, u32[]{:S(2)}, u32[]{:S(2)}) collective-permute-start(bf16[256,256]{1,0:T(8,128)(2,1)S(1)} %reduce_sum.51), channel_id=1, source_target_pairs={{0,4},{1,5},{2,6},{3,7},{4,0},{5,1},{6,2},{7,3},{8,12},{9,13},{10,... | collective-permute-start | bytes 393224 | tf_op jit(solution)/shard_map/ppermute | solution.py:186
  34.4 3.1 %collective-permute-start.1 = (bf16[256,256]{1,0:T(8,128)(2,1)S(1)}, bf16[256,256]{1,0:T(8,128)(2,1)S(1)}, u32[]{:S(2)}, u32[]{:S(2)}) collective-permute-start(bf16[256,256]{1,0:T(8,128)(2,1)S(1)} %reduce_sum.51), channel_id=1, source_target_pairs={{0,6},{1,7},{2,0},{3,1},{4,2},{5,3},{6,4},{7,5},{8,14},{9,15},{10,... | collective-permute-start | bytes 393224 | tf_op jit(solution)/shard_map/ppermute | solution.py:186
  37.4 0.6 all-to-all-done.1
  38.1 2.5 %collective-permute-start.3 = (bf16[256,256]{1,0:T(8,128)(2,1)S(1)}, bf16[256,256]{1,0:T(8,128)(2,1)S(1)}, u32[]{:S(2)}, u32[]{:S(2)}) collective-permute-start(bf16[256,256]{1,0:T(8,128)(2,1)S(1)} %reduce_sum.51), channel_id=1, source_target_pairs={{0,2},{1,3},{2,4},{3,5},{4,6},{5,7},{6,0},{7,1},{8,10},{9,11},{10,... | collective-permute-start | bytes 393224 | tf_op jit(solution)/shard_map/ppermute | solution.py:186
  40.6 0.7 broadcast_in_dim.4
  41.2 15.2 %all-to-all-start.2 = ((f32[16,8,256]{2,1,0:T(8,128)}), f32[16,8,256]{2,1,0:T(8,128)S(1)}, u32[]{:S(2)}, u32[]{:S(2)}) async-start(f32[16,8,256]{2,1,0:T(8,128)} %broadcast_in_dim.4), calls=%async_computation.2 | async-start | bytes 262144 | tf_op jit(solution)/shard_map/all_to_all | solution.py:27
  56.5 0.0 collective-permute-done.2
  56.5 0.0 collective-permute-done.1
  56.5 0.0 collective-permute-done.3
  56.5 0.1 pad_maximum_fusion.near_hbm
  56.6 1.9 %collective-permute-start.4 = (bf16[4,256,256]{2,1,0:T(8,128)(2,1)S(1)}, bf16[4,256,256]{2,1,0:T(8,128)(2,1)S(1)}, u32[]{:S(2)}, u32[]{:S(2)}) collective-permute-start(bf16[4,256,256]{2,1,0:T(8,128)(2,1)S(1)} %pad_maximum_fusion.near_hbm), channel_id=1, source_target_pairs={{0,1},{1,0},{2,3},{3,2},{4,5},{5,4},{6,7},{7,6},{8,9},{9,8},{10,11... | collective-permute-start | bytes 1572872 | tf_op jit(solution)/shard_map/ppermute | solution.py:216
  58.5 11.8 %all-to-all-done.2 = f32[16,8,256]{2,1,0:T(8,128)S(1)} async-done(((f32[16,8,256]{2,1,0:T(8,128)}), f32[16,8,256]{2,1,0:T(8,128)S(1)}, u32[]{:S(2)}, u32[]{:S(2)}) %all-to-all-start.2) | async-done | bytes 131104 | tf_op jit(solution)/shard_map/all_to_all | solution.py:27
  70.4 0.7 broadcast_in_dim.5
  71.1 5.9 %all-to-all-start.3 = ((f32[32,8,256]{2,1,0:T(8,128)}), f32[32,8,256]{2,1,0:T(8,128)S(1)}, u32[]{:S(2)}, u32[]{:S(2)}) async-start(f32[32,8,256]{2,1,0:T(8,128)} %broadcast_in_dim.5), calls=%async_computation.3 | async-start | bytes 524288 | tf_op jit(solution)/shard_map/all_to_all | solution.py:27
  77.0 0.0 collective-permute-done.4.far_hbm
  77.0 8.9 %all-to-all-done.3 = f32[32,8,256]{2,1,0:T(8,128)S(1)} async-done(((f32[32,8,256]{2,1,0:T(8,128)}), f32[32,8,256]{2,1,0:T(8,128)S(1)}, u32[]{:S(2)}, u32[]{:S(2)}) %all-to-all-start.3) | async-done | bytes 262176 | tf_op jit(solution)/shard_map/all_to_all | solution.py:27
  85.9 13.3 %project.1 = (bf16[32,2048]{1,0:T(8,128)(2,1)}, bf16[256,1024]{1,0:T(8,128)(2,1)S(1)}) custom-call(f32[256,256]{1,0:T(8,128)S(1)} %bitcast.17, bf16[4,256,256]{2,1,0:T(8,128)(2,1)S(1)} %pad_maximum_fusion.near_hbm, bf16[4,256,256]{2,1,0:T(8,128)(2,1)S(1)} %collective-permute-done.4.far_hbm, bf16[2048,1024]{1,0:T(8,128)(2,1)} %activations_hbm.1), custom_call_target="tpu_custom_call" | custom-call | tf_op jit(solution)/shard_map/project/pallas_call | solution.py:164
  99.2 12.6 %all_to_all.31 = bf16[4,64,1024]{2,1,0:T(8,128)(2,1)S(1)} all-to-all(bf16[4,64,1024]{2,1,0:T(8,128)(2,1)S(1)} %bitcast.18), channel_id=1, replica_groups={{0,8,16,24},{32,40,48,56},{64,72,80,88},{96,104,112,120},{128,136,144,1..., dimensions={0} | all-to-all | bytes 1048576 | tf_op jit(solution)/shard_map/all_to_all | solution.py:27
  111.8 0.1 reduce_sum.54
  111.8 0.1 reshape.23
  111.9 17.9 %all_to_all.32 = bf16[16,4,1024]{2,1,0:T(4,128)(2,1)S(1)} all-to-all(bf16[16,4,1024]{2,1,0:T(4,128)(2,1)S(1)} %reshape.23), channel_id=1, replica_groups={{0,32,64,96,128,160,192,224,256,288,320,352,384,416,448,480},{8,40,72,1..., dimensions={0} | all-to-all | bytes 262144 | tf_op jit(solution)/shard_map/all_to_all | solution.py:27
  129.8 0.7 convert_reduce_fusion
  (2 shorter events, 0.1 us)
Async XLA Ops:
  0.6 1.0 copy-start
  4.0 4.3 %collective-permute-start = (bf16[1024,256]{1,0:T(8,128)(2,1)S(1)}, bf16[1024,256]{1,0:T(8,128)(2,1)S(1)}, u32[]{:S(2)}, u32[]{:S(2)}) collective-permute-start(bf16[1024,256]{1,0:T(8,128)(2,1)S(1)} %fusion.4), channel_id=1, source_target_pairs={{0,1},{1,0},{2,3},{3,2},{4,5},{5,4},{6,7},{7,6},{8,9},{9,8},{10,11... | collective-permute-start | bytes 1572872 | tf_op jit(solution)/shard_map/ppermute | solution.py:203
  23.7 14.4 %all-to-all-start.1 = ((f32[32,8,256]{2,1,0:T(8,128)}), f32[32,8,256]{2,1,0:T(8,128)S(1)}, u32[]{:S(2)}, u32[]{:S(2)}) async-start(f32[32,8,256]{2,1,0:T(8,128)} %fusion.7), calls=%async_computation.1 | async-start | bytes 524288 | tf_op jit(solution)/shard_map/all_to_all | solution.py:27
  29.1 27.3 %collective-permute-start.2 = (bf16[256,256]{1,0:T(8,128)(2,1)S(1)}, bf16[256,256]{1,0:T(8,128)(2,1)S(1)}, u32[]{:S(2)}, u32[]{:S(2)}) collective-permute-start(bf16[256,256]{1,0:T(8,128)(2,1)S(1)} %reduce_sum.51), channel_id=1, source_target_pairs={{0,4},{1,5},{2,6},{3,7},{4,0},{5,1},{6,2},{7,3},{8,12},{9,13},{10,... | collective-permute-start | bytes 393224 | tf_op jit(solution)/shard_map/ppermute | solution.py:186
  34.4 22.1 %collective-permute-start.1 = (bf16[256,256]{1,0:T(8,128)(2,1)S(1)}, bf16[256,256]{1,0:T(8,128)(2,1)S(1)}, u32[]{:S(2)}, u32[]{:S(2)}) collective-permute-start(bf16[256,256]{1,0:T(8,128)(2,1)S(1)} %reduce_sum.51), channel_id=1, source_target_pairs={{0,6},{1,7},{2,0},{3,1},{4,2},{5,3},{6,4},{7,5},{8,14},{9,15},{10,... | collective-permute-start | bytes 393224 | tf_op jit(solution)/shard_map/ppermute | solution.py:186
  38.1 18.4 %collective-permute-start.3 = (bf16[256,256]{1,0:T(8,128)(2,1)S(1)}, bf16[256,256]{1,0:T(8,128)(2,1)S(1)}, u32[]{:S(2)}, u32[]{:S(2)}) collective-permute-start(bf16[256,256]{1,0:T(8,128)(2,1)S(1)} %reduce_sum.51), channel_id=1, source_target_pairs={{0,2},{1,3},{2,4},{3,5},{4,6},{5,7},{6,0},{7,1},{8,10},{9,11},{10,... | collective-permute-start | bytes 393224 | tf_op jit(solution)/shard_map/ppermute | solution.py:186
  41.2 29.1 %all-to-all-start.2 = ((f32[16,8,256]{2,1,0:T(8,128)}), f32[16,8,256]{2,1,0:T(8,128)S(1)}, u32[]{:S(2)}, u32[]{:S(2)}) async-start(f32[16,8,256]{2,1,0:T(8,128)} %broadcast_in_dim.4), calls=%async_computation.2 | async-start | bytes 262144 | tf_op jit(solution)/shard_map/all_to_all | solution.py:27
  56.6 20.4 %collective-permute-start.4 = (bf16[4,256,256]{2,1,0:T(8,128)(2,1)S(1)}, bf16[4,256,256]{2,1,0:T(8,128)(2,1)S(1)}, u32[]{:S(2)}, u32[]{:S(2)}) collective-permute-start(bf16[4,256,256]{2,1,0:T(8,128)(2,1)S(1)} %pad_maximum_fusion.near_hbm), channel_id=1, source_target_pairs={{0,1},{1,0},{2,3},{3,2},{4,5},{5,4},{6,7},{7,6},{8,9},{9,8},{10,11... | collective-permute-start | bytes 1572872 | tf_op jit(solution)/shard_map/ppermute | solution.py:216
  71.1 14.8 %all-to-all-start.3 = ((f32[32,8,256]{2,1,0:T(8,128)}), f32[32,8,256]{2,1,0:T(8,128)S(1)}, u32[]{:S(2)}, u32[]{:S(2)}) async-start(f32[32,8,256]{2,1,0:T(8,128)} %broadcast_in_dim.5), calls=%async_computation.3 | async-start | bytes 524288 | tf_op jit(solution)/shard_map/all_to_all | solution.py:27

commit v8 on v7

--- a/solution.py
+++ b/solution.py
@@ -118,7 +118,7 @@
     fetches = []
     for step in range(chips):
         for other, slices in enumerate((near_hbm, far_hbm)):
-            place = (core + other) % CORES * chips + (chip + step) % chips
+            place = (core + other) % CORES * chips + (chip ^ step)
             rows = pl.ds(pl.multiple_of(place * tokens, tokens), tokens)
             at = done.at[CORES * step + other]
             fetches.append(pltpu.make_async_copy(slices.at[step], sketch_ref.at[rows], at))
@@ -181,9 +181,8 @@
     )(gram, near, far, activations)
 
 
-def from_chip(own, step):
-    cols = lax.axis_size("col")
-    return lax.ppermute(own, "col", [(c, (c - CORES * step) % cols) for c in range(cols)])
+def swap(slices, distance):
+    return lax.ppermute(slices, "col", [(c, c ^ distance) for c in range(lax.axis_size("col"))])
 
 
 def local(activations, start_basis):
@@ -206,14 +205,15 @@
     partial = partial.reshape(cols // CORES, -1, rank)
     parts = exchange(partial, "col", along_x)
     own = jnp.sum(parts.astype(jnp.float32), 0).astype(jnp.bfloat16)
-    first_near = [own] + [from_chip(own, step) for step in range(1, cols // CORES - 1)]
+    near, distance = own[None], CORES
+    while distance < cols:
+        near = jnp.concatenate([near, swap(near, distance)])
+        distance *= 2
+    far = swap(near, 1)
 
     gram = lax.dot_general(own, own, (((0,), (0,)), ((), ())), preferred_element_type=jnp.float32)
     gram = gram.reshape(plane_size, rank // plane_size, rank)
     gram = jnp.sum(exchange(gram, ("row", "col"), plane), 0)
-    late, _ = lax.optimization_barrier((own, gram))
-    near = jnp.stack(first_near + [from_chip(late, cols // CORES - 1)])
-    far = lax.ppermute(near, "col", [(c, c ^ 1) for c in range(cols)])
     gram = jnp.sum(share(gram, depth, "row", along_z), 0)
     gram = share(gram, plane_size, ("row", "col"), plane).reshape(rank, rank)
 

time: 131 us -> 131 us (level)
  starting transfers between devices: 41.2 us -> 37 us
  waiting for transfers between devices: 21.4 us -> 25 us
    all_to_all x3, waiting for transfers between devices: 21.3 us -> 25 us  [exchange(): return lax.all_to_all(blocks, axis, 0, 0, axis_index_groups=members)]
    ppermute x4 -> x3, starting transfers between devices: 12.7 us -> 9.6 us  [swap(): lax.ppermute(slices, 'col', [(c, c ^ distance) for c in range(lax.axis_si...]
  transfers between devices with their start and end apart: 8 -> 7, of which waited for: 3 -> 3; matrix products, arithmetic and copies ran while one was open for 3% -> 4% of each run, Pallas kernels for 0% -> 0%
where the time goes in v8:
time: 131 us; the launch traced here: 130 us
  blocking collectives  45 us (34%)
  starting transfers between devices  37 us (28%)
  waiting for transfers between devices  25 us (19%)
  Pallas kernels  13.3 us (10%)
  matrix products  5.49 us (4%)
  local copies, waits for them, and re-layouts  2.56 us (2%)
    all_to_all x3, blocking collectives, exchange(): return lax.all_to_all(blocks, axis, 0, 0, axis_index_groups=members)  45 us
    all_to_all x3, starting transfers between devices, exchange(): return lax.all_to_all(blocks, axis, 0, 0, axis_index_groups=members)  25.4 us
    all_to_all x3, waiting for transfers between devices, exchange(): return lax.all_to_all(blocks, axis, 0, 0, axis_index_groups=members)  25 us
    pallas_call x1, Pallas kernels, project(): pl.pallas_call(functools.partial(project_kernel, scale=scale, depth=depth...  13.3 us
    ppermute x3, starting transfers between devices, swap(): lax.ppermute(slices, 'col', [(c, c ^ distance) for c in range(lax.axis_si...  9.6 us
    dot_general x2, matrix products, half_sketch(): return jnp.dot(block, start_basis, preferred_element_type=jnp.float32)  4.6 us
  transfers between devices with their start and end apart: 7, of which 3 were waited for; matrix products, arithmetic and copies ran while one was open for 4% of the time, Pallas kernels for 0%

profile of v8, /device:TPU:32, one launch (start us, length us, event | category | flops | bytes accessed | tf_op | source)
XLA Modules:
  0.0 130.2 jit_solution(18209402058938355087)
XLA Ops:
  0.6 0.0 copy-start
  0.7 1.0 copy-done
  1.7 2.3 %fusion.4 = bf16[1024,256]{1,0:T(8,128)(2,1)S(1)} fusion(bf16[1024,256]{1,0:T(8,128)(2,1)S(1)} %copy-done, bf16[2048,1024]{1,0:T(8,128)(2,1)} %activations_hbm.1, s32[]{:T(128)S(6)} %select_n.15), kind=kOutput, calls=%fused_computation.4 | convolution fusion | flops 537133056 | bytes 3145732 | tf_op jit(solution)/shard_map/dot_general | solution.py:199
  4.0 1.9 %collective-permute-start = (bf16[1024,256]{1,0:T(8,128)(2,1)S(1)}, bf16[1024,256]{1,0:T(8,128)(2,1)S(1)}, u32[]{:S(2)}, u32[]{:S(2)}) collective-permute-start(bf16[1024,256]{1,0:T(8,128)(2,1)S(1)} %fusion.4), channel_id=1, source_target_pairs={{0,1},{1,0},{2,3},{3,2},{4,5},{5,4},{6,7},{7,6},{8,9},{9,8},{10,11... | collective-permute-start | bytes 1572872 | tf_op jit(solution)/shard_map/ppermute | solution.py:202
  5.9 2.3 %fusion.2 = f32[1024,256]{1,0:T(8,128)S(1)} fusion(bf16[1024,256]{1,0:T(8,128)(2,1)S(1)} %copy-done, bf16[2048,1024]{1,0:T(8,128)(2,1)} %activations_hbm.1, s32[]{:T(128)S(6)} %select_n.14), kind=kOutput, calls=%fused_computation.2 | convolution fusion | flops 536870912 | bytes 3670020 | tf_op jit(solution)/shard_map/dot_general | solution.py:199
  8.2 0.0 collective-permute-done
  8.2 0.1 add_convert_fusion
  8.4 14.2 %all_to_all.30 = bf16[4,256,256]{2,1,0:T(8,128)(2,1)S(1)} all-to-all(bf16[4,256,256]{2,1,0:T(8,128)(2,1)S(1)} %bitcast.20), channel_id=1, replica_groups={{0,2,4,6},{1,3,5,7},{8,10,12,14},{9,11,13,15},{16,18,20,22},{17,19,21,2..., dimensions={0} | all-to-all | bytes 1048576 | tf_op jit(solution)/shard_map/all_to_all | solution.py:27
  22.6 0.1 reduce_sum.51
  22.7 0.1 copy.11
  22.8 2.5 %collective-permute-start.1 = (bf16[1,256,256]{2,1,0:T(8,128)(2,1)S(1)}, bf16[1,256,256]{2,1,0:T(8,128)(2,1)S(1)}, u32[]{:S(2)}, u32[]{:S(2)}) collective-permute-start(bf16[1,256,256]{2,1,0:T(8,128)(2,1)S(1)} %bitcast.17), channel_id=1, source_target_pairs={{0,2},{1,3},{2,0},{3,1},{4,6},{5,7},{6,4},{7,5},{8,10},{9,11},{10,... | collective-permute-start | bytes 393224 | tf_op jit(solution)/shard_map/ppermute | solution.py:185
  25.3 0.9 fusion.7
  26.2 6.4 %all-to-all-start.1 = ((f32[32,8,256]{2,1,0:T(8,128)}), f32[32,8,256]{2,1,0:T(8,128)S(1)}, u32[]{:S(2)}, u32[]{:S(2)}) async-start(f32[32,8,256]{2,1,0:T(8,128)} %fusion.7), calls=%async_computation.1 | async-start | bytes 524288 | tf_op jit(solution)/shard_map/all_to_all | solution.py:27
  32.5 0.0 collective-permute-done.1
  32.6 5.2 %collective-permute-start.2 = (bf16[2,256,256]{2,1,0:T(8,128)(2,1)S(1)}, bf16[2,256,256]{2,1,0:T(8,128)(2,1)S(1)}, u32[]{:S(2)}, u32[]{:S(2)}) collective-permute-start(bf16[2,256,256]{2,1,0:T(8,128)(2,1)S(1)} %pad_maximum_fusion.1), channel_id=1, source_target_pairs={{0,4},{1,5},{2,6},{3,7},{4,0},{5,1},{6,2},{7,3},{8,12},{9,13},{10,... | collective-permute-start | bytes 786440 | tf_op jit(solution)/shard_map/ppermute | solution.py:185
  37.8 3.6 %all-to-all-done.1 = f32[32,8,256]{2,1,0:T(8,128)S(1)} async-done(((f32[32,8,256]{2,1,0:T(8,128)}), f32[32,8,256]{2,1,0:T(8,128)S(1)}, u32[]{:S(2)}, u32[]{:S(2)}) %all-to-all-start.1) | async-done | bytes 262176 | tf_op jit(solution)/shard_map/all_to_all | solution.py:27
  41.5 0.7 broadcast_in_dim.6
  42.1 15.2 %all-to-all-start.2 = ((f32[16,8,256]{2,1,0:T(8,128)}), f32[16,8,256]{2,1,0:T(8,128)S(1)}, u32[]{:S(2)}, u32[]{:S(2)}) async-start(f32[16,8,256]{2,1,0:T(8,128)} %broadcast_in_dim.6), calls=%async_computation.2 | async-start | bytes 262144 | tf_op jit(solution)/shard_map/all_to_all | solution.py:27
  57.3 0.0 collective-permute-done.2
  57.3 0.1 pad_maximum_fusion.near_hbm
  57.4 1.9 %collective-permute-start.3 = (bf16[4,256,256]{2,1,0:T(8,128)(2,1)S(1)}, bf16[4,256,256]{2,1,0:T(8,128)(2,1)S(1)}, u32[]{:S(2)}, u32[]{:S(2)}) collective-permute-start(bf16[4,256,256]{2,1,0:T(8,128)(2,1)S(1)} %pad_maximum_fusion.near_hbm), channel_id=1, source_target_pairs={{0,1},{1,0},{2,3},{3,2},{4,5},{5,4},{6,7},{7,6},{8,9},{9,8},{10,11... | collective-permute-start | bytes 1572872 | tf_op jit(solution)/shard_map/ppermute | solution.py:185
  59.3 12.5 %all-to-all-done.2 = f32[16,8,256]{2,1,0:T(8,128)S(1)} async-done(((f32[16,8,256]{2,1,0:T(8,128)}), f32[16,8,256]{2,1,0:T(8,128)S(1)}, u32[]{:S(2)}, u32[]{:S(2)}) %all-to-all-start.2) | async-done | bytes 131104 | tf_op jit(solution)/shard_map/all_to_all | solution.py:27
  71.8 0.7 broadcast_in_dim.7
  72.5 3.9 %all-to-all-start.3 = ((f32[32,8,256]{2,1,0:T(8,128)}), f32[32,8,256]{2,1,0:T(8,128)S(1)}, u32[]{:S(2)}, u32[]{:S(2)}) async-start(f32[32,8,256]{2,1,0:T(8,128)} %broadcast_in_dim.7), calls=%async_computation.3 | async-start | bytes 524288 | tf_op jit(solution)/shard_map/all_to_all | solution.py:27
  76.4 0.0 collective-permute-done.3.far_hbm
  76.4 8.9 %all-to-all-done.3 = f32[32,8,256]{2,1,0:T(8,128)S(1)} async-done(((f32[32,8,256]{2,1,0:T(8,128)}), f32[32,8,256]{2,1,0:T(8,128)S(1)}, u32[]{:S(2)}, u32[]{:S(2)}) %all-to-all-start.3) | async-done | bytes 262176 | tf_op jit(solution)/shard_map/all_to_all | solution.py:27
  85.3 13.3 %project.1 = (bf16[32,2048]{1,0:T(8,128)(2,1)}, bf16[256,1024]{1,0:T(8,128)(2,1)S(1)}) custom-call(f32[256,256]{1,0:T(8,128)S(1)} %bitcast.14, bf16[4,256,256]{2,1,0:T(8,128)(2,1)S(1)} %pad_maximum_fusion.near_hbm, bf16[4,256,256]{2,1,0:T(8,128)(2,1)S(1)} %collective-permute-done.3.far_hbm, bf16[2048,1024]{1,0:T(8,128)(2,1)} %activations_hbm.1), custom_call_target="tpu_custom_call" | custom-call | tf_op jit(solution)/shard_map/project/pallas_call | solution.py:164
  98.6 12.6 %all_to_all.31 = bf16[4,64,1024]{2,1,0:T(8,128)(2,1)S(1)} all-to-all(bf16[4,64,1024]{2,1,0:T(8,128)(2,1)S(1)} %bitcast.15), channel_id=1, replica_groups={{0,8,16,24},{32,40,48,56},{64,72,80,88},{96,104,112,120},{128,136,144,1..., dimensions={0} | all-to-all | bytes 1048576 | tf_op jit(solution)/shard_map/all_to_all | solution.py:27
  111.2 0.1 reduce_sum.54
  111.3 0.1 reshape.23
  111.3 18.1 %all_to_all.32 = bf16[16,4,1024]{2,1,0:T(4,128)(2,1)S(1)} all-to-all(bf16[16,4,1024]{2,1,0:T(4,128)(2,1)S(1)} %reshape.23), channel_id=1, replica_groups={{0,32,64,96,128,160,192,224,256,288,320,352,384,416,448,480},{8,40,72,1..., dimensions={0} | all-to-all | bytes 262144 | tf_op jit(solution)/shard_map/all_to_all | solution.py:27
  129.5 0.7 convert_reduce_fusion
  (3 shorter events, 0.1 us)
Async XLA Ops:
  0.6 1.0 copy-start
  4.0 4.3 %collective-permute-start = (bf16[1024,256]{1,0:T(8,128)(2,1)S(1)}, bf16[1024,256]{1,0:T(8,128)(2,1)S(1)}, u32[]{:S(2)}, u32[]{:S(2)}) collective-permute-start(bf16[1024,256]{1,0:T(8,128)(2,1)S(1)} %fusion.4), channel_id=1, source_target_pairs={{0,1},{1,0},{2,3},{3,2},{4,5},{5,4},{6,7},{7,6},{8,9},{9,8},{10,11... | collective-permute-start | bytes 1572872 | tf_op jit(solution)/shard_map/ppermute | solution.py:202
  22.8 9.7 %collective-permute-start.1 = (bf16[1,256,256]{2,1,0:T(8,128)(2,1)S(1)}, bf16[1,256,256]{2,1,0:T(8,128)(2,1)S(1)}, u32[]{:S(2)}, u32[]{:S(2)}) collective-permute-start(bf16[1,256,256]{2,1,0:T(8,128)(2,1)S(1)} %bitcast.17), channel_id=1, source_target_pairs={{0,2},{1,3},{2,0},{3,1},{4,6},{5,7},{6,4},{7,5},{8,10},{9,11},{10,... | collective-permute-start | bytes 393224 | tf_op jit(solution)/shard_map/ppermute | solution.py:185
  26.2 15.3 %all-to-all-start.1 = ((f32[32,8,256]{2,1,0:T(8,128)}), f32[32,8,256]{2,1,0:T(8,128)S(1)}, u32[]{:S(2)}, u32[]{:S(2)}) async-start(f32[32,8,256]{2,1,0:T(8,128)} %fusion.7), calls=%async_computation.1 | async-start | bytes 524288 | tf_op jit(solution)/shard_map/all_to_all | solution.py:27
  32.6 24.8 %collective-permute-start.2 = (bf16[2,256,256]{2,1,0:T(8,128)(2,1)S(1)}, bf16[2,256,256]{2,1,0:T(8,128)(2,1)S(1)}, u32[]{:S(2)}, u32[]{:S(2)}) collective-permute-start(bf16[2,256,256]{2,1,0:T(8,128)(2,1)S(1)} %pad_maximum_fusion.1), channel_id=1, source_target_pairs={{0,4},{1,5},{2,6},{3,7},{4,0},{5,1},{6,2},{7,3},{8,12},{9,13},{10,... | collective-permute-start | bytes 786440 | tf_op jit(solution)/shard_map/ppermute | solution.py:185
  42.1 29.7 %all-to-all-start.2 = ((f32[16,8,256]{2,1,0:T(8,128)}), f32[16,8,256]{2,1,0:T(8,128)S(1)}, u32[]{:S(2)}, u32[]{:S(2)}) async-start(f32[16,8,256]{2,1,0:T(8,128)} %broadcast_in_dim.6), calls=%async_computation.2 | async-start | bytes 262144 | tf_op jit(solution)/shard_map/all_to_all | solution.py:27
  57.4 19.0 %collective-permute-start.3 = (bf16[4,256,256]{2,1,0:T(8,128)(2,1)S(1)}, bf16[4,256,256]{2,1,0:T(8,128)(2,1)S(1)}, u32[]{:S(2)}, u32[]{:S(2)}) collective-permute-start(bf16[4,256,256]{2,1,0:T(8,128)(2,1)S(1)} %pad_maximum_fusion.near_hbm), channel_id=1, source_target_pairs={{0,1},{1,0},{2,3},{3,2},{4,5},{5,4},{6,7},{7,6},{8,9},{9,8},{10,11... | collective-permute-start | bytes 1572872 | tf_op jit(solution)/shard_map/ppermute | solution.py:185
  72.5 12.8 %all-to-all-start.3 = ((f32[32,8,256]{2,1,0:T(8,128)}), f32[32,8,256]{2,1,0:T(8,128)S(1)}, u32[]{:S(2)}, u32[]{:S(2)}) async-start(f32[32,8,256]{2,1,0:T(8,128)} %broadcast_in_dim.7), calls=%async_computation.3 | async-start | bytes 524288 | tf_op jit(solution)/shard_map/all_to_all | solution.py:27
